TPU v7x, 128 devices: a whole 4x4x4 slice. The times are simulated.
128 devices in a mesh: leaf: 16 (over x_lo, z, core), sub: 8 (over x_hi, y).
Axes of the slice: x: 4 (x_hi: 2, x_lo: 2; x = x_hi * 2 + x_lo), y: 4, z: 4, core: 2. Of those that a mesh axis runs over, the one named last changes fastest.
Arguments:
- density: bfloat16 [32, 2097152], P(None, ('leaf', 'sub')), may hold values from -6 to 6
- geometry: float32 [8192, 6, 256], P(('leaf', 'sub')), may hold values from -134 to 134
- near_list: int32 [8192, 9], P(('leaf', 'sub')), may hold values from 0 to 8191, as said below
- near_count: int32 [8192], P(('leaf', 'sub')), may hold values from 1 to 9, as said below
- far_list: int32 [8192, 16], P(('leaf', 'sub')), may hold values from 0 to 8191, as said below
- bases: bfloat16 [8192, 64, 256], P(('leaf', 'sub')), may hold values from -0.375 to 0.375
- proxies: float32 [8192, 3, 64], P(('leaf', 'sub')), may hold values from -134 to 134
- leaf_transfer: bfloat16 [8192, 64, 64], P(('leaf', 'sub')), may hold values from -0.25 to 0.25
- parent_transfer: bfloat16 [1024, 64, 64], P(('leaf', 'sub')), may hold values from -0.75 to 0.75
- top_proxies: float32 [16, 3, 64], replicated, may hold values from -4 to 4
- top_far: int32 [16, 8], replicated, may hold values from 0 to 15, as said below
Outputs:
- product: float32 [32, 2097152], P(None, ('leaf', 'sub'))
Inputs may be any that keep to these rules, and one draw needn't show every extreme that they name: `near_list`: slot 0 of row t is t itself; the other slots hold, in an order drawn for each leaf, the eight leaves t + a * 31 + b modulo 8192 with a and b each -1, 0 or 1, not both 0. `near_count`: the live slots on the leaves of one device number at most 416 together, and exactly 416 on one device. `far_list`: row t holds sixteen distinct leaves, in an order drawn for each leaf, chosen for each leaf from the twenty-two leaves t + a * 31 + b modulo 8192 with a from -2 to 2, b from -3 to 3, and either the larger of |a| and |b| equal to 2, or |a| at most 1 and |b| equal to 3. `top_far`: distinct nodes, none equal to the node or to its two cyclic neighbours.
All inputs are finite; a program needn't handle non-finite values.
Results may differ from a plain program's by a relative error of at most 0.007.
Values may be sent and summed in bfloat16 or wider, within the bound.
No kernel may reach another device: no remote copies, remote signals or barrier semaphores. Data moves between devices by JAX's collectives and lax.ppermute only.
A program may use at most 64 MiB of HBM per device.

v0:
```python
import math

import jax
import jax.numpy as jnp
from jax import lax
from jax.sharding import PartitionSpec as P

SOFTEN = 0.01
FOUR_PI = 4.0 * math.pi


def padded(block, sides, width):
    for axis, dim in sides:
        count = lax.axis_size(axis)
        forward = [(i, i + 1) for i in range(count - 1)]
        forward.append((count - 1, 0))
        backward = [(target, source) for source, target in forward]
        low = lax.ppermute(
            lax.slice_in_dim(block, block.shape[dim] - width, None, axis=dim), axis, forward
        )
        high = lax.ppermute(lax.slice_in_dim(block, 0, width, axis=dim), axis, backward)
        block = jnp.concatenate([low, block, high], axis=dim)
    return block


def gaps(targets, sources):
    differ_one = targets[..., 0, None, :] - sources[..., 0, :, None]
    differ_two = targets[..., 1, None, :] - sources[..., 1, :, None]
    differ_three = targets[..., 2, None, :] - sources[..., 2, :, None]
    squared = (
        differ_one * differ_one + differ_two * differ_two + differ_three * differ_three + SOFTEN
    )
    return (differ_one, differ_two, differ_three, squared)


def pair_kernel(targets, sources, normals):
    differ_one, differ_two, differ_three, squared = gaps(targets, sources)
    flux = (
        normals[..., 0, :, None] * differ_one
        + normals[..., 1, :, None] * differ_two
        + normals[..., 2, :, None] * differ_three
    )
    return flux / (FOUR_PI * squared * jnp.sqrt(squared))


def proxy_kernel(targets, sources):
    squared = gaps(targets, sources)[3]
    return 1.0 / (FOUR_PI * jnp.sqrt(squared))


def local_index(global_ids, first_leaf, leaf_count, total_leaves, reach):
    own_rows = jnp.arange(leaf_count, dtype=jnp.int32)[:, None]
    half_total = total_leaves // 2
    offset = (global_ids - (first_leaf + own_rows) + half_total) % total_leaves - half_total
    return own_rows + reach + offset


def per_device(
    density,
    geometry,
    near_list,
    near_count,
    far_list,
    bases,
    proxies,
    leaf_transfer,
    parent_transfer,
    top_proxies,
    top_far,
):
    leaf_count = geometry.shape[0]
    sides = density.shape[0]
    leaf_width = geometry.shape[2]
    rank_size = bases.shape[1]
    slots = near_list.shape[1]
    total_leaves = leaf_count * lax.axis_size(("leaf", "sub"))
    first_leaf = lax.axis_index(("leaf", "sub")) * leaf_count
    plain = density.reshape(sides, leaf_count, leaf_width)
    coefficients = jnp.einsum(
        "nlp,lrp->nlr", plain, bases, preferred_element_type=jnp.float32
    ).astype(jnp.bfloat16)
    flat_geometry = jnp.concatenate(
        [geometry.reshape(leaf_count, 6 * leaf_width), proxies.reshape(leaf_count, 3 * rank_size)],
        axis=1,
    )
    geometry_all = padded(flat_geometry, ((("leaf", "sub"), 0),), leaf_count)
    source_geometry = geometry_all[:, : 6 * leaf_width].reshape(-1, 6, leaf_width)
    source_proxies = geometry_all[:, 6 * leaf_width :].reshape(-1, 3, rank_size)
    density_reach = leaf_count // 2
    density_all = padded(density, ((("leaf", "sub"), 1),), density_reach * leaf_width).reshape(
        sides, -1, leaf_width
    )
    coeff_flat = coefficients.reshape(sides, leaf_count * rank_size)
    coeff_all = padded(coeff_flat, ((("leaf", "sub"), 1),), leaf_count * rank_size).reshape(
        sides, -1, rank_size
    )
    targets = jnp.repeat(jnp.arange(leaf_count, dtype=jnp.int32), slots)
    geo_sources = local_index(near_list, first_leaf, leaf_count, total_leaves, leaf_count).reshape(
        -1
    )
    den_sources = geo_sources - (leaf_count - density_reach)
    live_mask = (jnp.arange(slots, dtype=jnp.int32)[None, :] < near_count[:, None]).reshape(-1)
    block_size = 4 * slots
    weights = live_mask.astype(jnp.float32)
    pair_count = targets.shape[0]
    step_count = pair_count // block_size

    def near_step(totals, items):
        block_targets, block_geo, block_den, block_weights = items
        target_pos = geometry[block_targets, :3]
        source_geo = source_geometry[block_geo]
        kernel = pair_kernel(target_pos, source_geo[:, :3], source_geo[:, 3:]).astype(jnp.bfloat16)
        source_density = density_all[:, block_den]
        partial_value = jnp.einsum(
            "nbs,bst->nbt", source_density, kernel, preferred_element_type=jnp.float32
        )
        partial_value = partial_value * block_weights[None, :, None]
        return (totals.at[:, block_targets].add(partial_value), None)

    start_totals = jnp.zeros((sides, leaf_count, leaf_width), jnp.float32)
    near_field, _ = lax.scan(
        near_step,
        start_totals,
        (
            targets.reshape(step_count, block_size),
            geo_sources.reshape(step_count, block_size),
            den_sources.reshape(step_count, block_size),
            weights.reshape(step_count, block_size),
        ),
    )
    far_sources = local_index(far_list, first_leaf, leaf_count, total_leaves, leaf_count)
    far_kernel = proxy_kernel(proxies[:, None], source_proxies[far_sources]).astype(jnp.bfloat16)
    leaf_far = jnp.einsum(
        "nlfs,lfst->nlt", coeff_all[:, far_sources], far_kernel, preferred_element_type=jnp.float32
    )
    lifted = jnp.einsum(
        "nlr,lrs->nls", coefficients, leaf_transfer, preferred_element_type=jnp.float32
    )
    parent_coefficients = jnp.sum(
        lifted.reshape(sides, leaf_count // 8, 8, rank_size), axis=2
    ).astype(jnp.bfloat16)
    partial_top = jnp.einsum(
        "npr,prs->ns", parent_coefficients, parent_transfer, preferred_element_type=jnp.float32
    )
    group_total = lax.psum(partial_top, "sub").astype(jnp.bfloat16)
    coupled = lax.all_gather(group_total[None], "leaf", axis=0, tiled=True)
    my_group = lax.axis_index("leaf")
    far_nodes = top_far[my_group]
    top_kernel = proxy_kernel(top_proxies[my_group][None], top_proxies[far_nodes]).astype(
        jnp.bfloat16
    )
    top_local = jnp.einsum(
        "kns,kst->nt", coupled[far_nodes], top_kernel, preferred_element_type=jnp.float32
    ).astype(jnp.bfloat16)
    parent_local = jnp.einsum(
        "ns,prs->npr", top_local, parent_transfer, preferred_element_type=jnp.float32
    ).astype(jnp.bfloat16)
    spread_parent = jnp.repeat(parent_local, 8, axis=1)
    leaf_local = jnp.einsum(
        "nls,lrs->nlr", spread_parent, leaf_transfer, preferred_element_type=jnp.float32
    )
    leaf_local = (leaf_local + leaf_far).astype(jnp.bfloat16)
    product = 0.5 * plain.astype(jnp.float32) + near_field
    product = product + jnp.einsum(
        "nlr,lrp->nlp", leaf_local, bases, preferred_element_type=jnp.float32
    )
    return product.reshape(sides, leaf_count * leaf_width)


def solution(mesh):
    placed = (
        P(None, ("leaf", "sub")),
        P(("leaf", "sub"), None, None),
        P(("leaf", "sub"), None),
        P(("leaf", "sub")),
        P(("leaf", "sub"), None),
        P(("leaf", "sub"), None, None),
        P(("leaf", "sub"), None, None),
        P(("leaf", "sub"), None, None),
        P(("leaf", "sub"), None, None),
        P(),
        P(),
    )
    return jax.shard_map(
        per_device, mesh=mesh, in_specs=placed, out_specs=P(None, ("leaf", "sub")), check_vma=False
    )
```

profile of v0, /device:TPU:8, one launch (start us, length us, event | category | flops | bytes accessed | tf_op | source)
XLA Modules:
  0.0 724.3 jit_solution(13661018172748555345)
XLA Ops:
  43.2 40.7 %psum.7 = bf16[32,64]{1,0:T(8,128)(2,1)} all-reduce(f32[32,64]{1,0:T(8,128)} %convolution_bitcast_fusion.2), channel_id=1, replica_groups=mesh['leaf'=16,'sub'=8] {'sub'}, use_global_device_ids=true, to_apply=%region_4.5 | all-reduce | flops 2048 | bytes 12288 | tf_op jit(solution)/shard_map/psum | solution.py:145
  83.9 20.7 %all-gather = bf16[512,64]{1,0:T(8,128)(2,1)} all-gather(bf16[32,64]{1,0:T(8,128)(2,1)} %psum.7), channel_id=2, replica_groups=mesh['leaf'=16,'sub'=8] {'leaf'}, dimensions={0}, use_global_device_ids=true | all-gather | bytes 69632 | tf_op jit(solution)/shard_map/all_gather | solution.py:146
  128.0 11.3 %gather_fusion.6 = bf16[1024,32,64]{2,1,0:T(8,128)(2,1)} fusion(bf16[32,192,64]{2,0,1:T(8,128)(2,1)} %pad_maximum_fusion.1, s32[1024]{0:T(1024)S(1)} %broadcast_clamp_fusion), kind=kCustom, calls=%fused_computation.6 | custom fusion | bytes 8392704 | tf_op jit(solution)/shard_map/gather | solution.py:134
  143.8 7.9 %gather_fusion.5 = f32[1024,3,64]{2,1,0:T(4,128)} fusion(f32[192,3,64]{2,1,0:T(4,128)S(1)} %copy.40, s32[1024]{0:T(1024)S(1)} %broadcast_clamp_fusion), kind=kCustom, calls=%fused_computation.5 | custom fusion | bytes 1576960 | tf_op jit(solution)/shard_map/gather | solution.py:132
  153.6 35.6 %fusion.27 = f32[32,64,64]{2,0,1:T(8,128)} fusion(bf16[32,64,16,64]{3,0,2,1:T(8,128)(2,1)} %bitcast.187, f32[64,16,64]{2,1,0:T(8,128)S(1)} %get-tuple-element.95, f32[64,64]{1,0:T(8,128)S(1)} %copy-done.7, f32[64,16,64]{2,1,0:T(8,128)S(1)} %get-tuple-element.94, f32[64,64]{1,0:T(8,128)S(1)} %copy-done.8, f32[64,16,64]{2,1,0:T(8,128)S(1)} %get-tuple-element.93, ...), kind=kOutput, calls=%fused_computation.62 | convolution fusion | flops 318767104 | bytes 5554176 | tf_op jit(solution)/shard_map/nlfs,lfst->nlt/dot_general | solution.py:133
  198.8 516.6 %while.10 = (s32[]{:T(128)}, f32[32,64,256]{2,0,1:T(8,128)}, s32[16,36]{1,0:T(8,128)}, s32[16,36]{1,0:T(8,128)S(1)}, f32[192,6,256]{2,1,0:T(8,128)}, /*index=5*/...) while((s32[]{:T(128)}, f32[32,64,256]{2,0,1:T(8,128)}, ...), condition=%wide.region_2.3_spmd, body=%wide.region_0.2_spmd.sunk | while | flops 194054544 | bytes 8600065 | solution.py:121
  208.8 14.8 %fusion.97 = f32[36,32,256]{2,1,0:T(8,128)S(1)} fusion(f32[36,256]{1,0:T(8,128)S(1)} %bitcast.194, f32[36,256]{1,0:T(8,128)} %get-tuple-element.181, f32[36,256]{1,0:T(8,128)S(1)} %bitcast.195, f32[36,256]{1,0:T(8,128)S(1)} %bitcast.196, f32[36,256]{1,0:T(8,128)} %get-tuple-element.184, f32[36,256]{1,0:T(8,128)S(1)} %bitcast.197, ...), kind=kOutput, calls=%fused_computation.23.clone.1 | convolution fusion | flops 193757184 | bytes 2101392 | tf_op jit(solution)/shard_map/while/body/eval_jaxpr/nbs,bst->nbt/dot_general | solution.py:114
  241.0 14.8 %fusion.97 = f32[36,32,256]{2,1,0:T(8,128)S(1)} fusion(f32[36,256]{1,0:T(8,128)S(1)} %bitcast.194, f32[36,256]{1,0:T(8,128)} %get-tuple-element.181, f32[36,256]{1,0:T(8,128)S(1)} %bitcast.195, f32[36,256]{1,0:T(8,128)S(1)} %bitcast.196, f32[36,256]{1,0:T(8,128)} %get-tuple-element.184, f32[36,256]{1,0:T(8,128)S(1)} %bitcast.197, ...), kind=kOutput, calls=%fused_computation.23.clone.1 | convolution fusion | flops 193757184 | bytes 2101392 | tf_op jit(solution)/shard_map/while/body/eval_jaxpr/nbs,bst->nbt/dot_general | solution.py:114
  273.3 14.8 %fusion.97 = f32[36,32,256]{2,1,0:T(8,128)S(1)} fusion(f32[36,256]{1,0:T(8,128)S(1)} %bitcast.194, f32[36,256]{1,0:T(8,128)} %get-tuple-element.181, f32[36,256]{1,0:T(8,128)S(1)} %bitcast.195, f32[36,256]{1,0:T(8,128)S(1)} %bitcast.196, f32[36,256]{1,0:T(8,128)} %get-tuple-element.184, f32[36,256]{1,0:T(8,128)S(1)} %bitcast.197, ...), kind=kOutput, calls=%fused_computation.23.clone.1 | convolution fusion | flops 193757184 | bytes 2101392 | tf_op jit(solution)/shard_map/while/body/eval_jaxpr/nbs,bst->nbt/dot_general | solution.py:114
  305.5 14.8 %fusion.97 = f32[36,32,256]{2,1,0:T(8,128)S(1)} fusion(f32[36,256]{1,0:T(8,128)S(1)} %bitcast.194, f32[36,256]{1,0:T(8,128)} %get-tuple-element.181, f32[36,256]{1,0:T(8,128)S(1)} %bitcast.195, f32[36,256]{1,0:T(8,128)S(1)} %bitcast.196, f32[36,256]{1,0:T(8,128)} %get-tuple-element.184, f32[36,256]{1,0:T(8,128)S(1)} %bitcast.197, ...), kind=kOutput, calls=%fused_computation.23.clone.1 | convolution fusion | flops 193757184 | bytes 2101392 | tf_op jit(solution)/shard_map/while/body/eval_jaxpr/nbs,bst->nbt/dot_general | solution.py:114
  337.8 14.8 %fusion.97 = f32[36,32,256]{2,1,0:T(8,128)S(1)} fusion(f32[36,256]{1,0:T(8,128)S(1)} %bitcast.194, f32[36,256]{1,0:T(8,128)} %get-tuple-element.181, f32[36,256]{1,0:T(8,128)S(1)} %bitcast.195, f32[36,256]{1,0:T(8,128)S(1)} %bitcast.196, f32[36,256]{1,0:T(8,128)} %get-tuple-element.184, f32[36,256]{1,0:T(8,128)S(1)} %bitcast.197, ...), kind=kOutput, calls=%fused_computation.23.clone.1 | convolution fusion | flops 193757184 | bytes 2101392 | tf_op jit(solution)/shard_map/while/body/eval_jaxpr/nbs,bst->nbt/dot_general | solution.py:114
  370.0 14.8 %fusion.97 = f32[36,32,256]{2,1,0:T(8,128)S(1)} fusion(f32[36,256]{1,0:T(8,128)S(1)} %bitcast.194, f32[36,256]{1,0:T(8,128)} %get-tuple-element.181, f32[36,256]{1,0:T(8,128)S(1)} %bitcast.195, f32[36,256]{1,0:T(8,128)S(1)} %bitcast.196, f32[36,256]{1,0:T(8,128)} %get-tuple-element.184, f32[36,256]{1,0:T(8,128)S(1)} %bitcast.197, ...), kind=kOutput, calls=%fused_computation.23.clone.1 | convolution fusion | flops 193757184 | bytes 2101392 | tf_op jit(solution)/shard_map/while/body/eval_jaxpr/nbs,bst->nbt/dot_general | solution.py:114
  402.2 14.8 %fusion.97 = f32[36,32,256]{2,1,0:T(8,128)S(1)} fusion(f32[36,256]{1,0:T(8,128)S(1)} %bitcast.194, f32[36,256]{1,0:T(8,128)} %get-tuple-element.181, f32[36,256]{1,0:T(8,128)S(1)} %bitcast.195, f32[36,256]{1,0:T(8,128)S(1)} %bitcast.196, f32[36,256]{1,0:T(8,128)} %get-tuple-element.184, f32[36,256]{1,0:T(8,128)S(1)} %bitcast.197, ...), kind=kOutput, calls=%fused_computation.23.clone.1 | convolution fusion | flops 193757184 | bytes 2101392 | tf_op jit(solution)/shard_map/while/body/eval_jaxpr/nbs,bst->nbt/dot_general | solution.py:114
  416.9 7.7 %scatter_fusion = f32[32,64,256]{2,0,1:T(8,128)} fusion(f32[32,64,256]{2,0,1:T(8,128)} %get-tuple-element.201, s32[36]{0:T(128)S(1)} %bitcast.204, f32[36,32,256]{2,1,0:T(8,128)S(1)} %fusion.97), kind=kCustom, calls=%fused_computation.7.clone.1 | custom fusion | flops 294912 | bytes 3539088 | tf_op jit(solution)/shard_map/while/body/eval_jaxpr/scatter-add | solution.py:118
  434.7 14.8 %fusion.97 = f32[36,32,256]{2,1,0:T(8,128)S(1)} fusion(f32[36,256]{1,0:T(8,128)S(1)} %bitcast.194, f32[36,256]{1,0:T(8,128)} %get-tuple-element.181, f32[36,256]{1,0:T(8,128)S(1)} %bitcast.195, f32[36,256]{1,0:T(8,128)S(1)} %bitcast.196, f32[36,256]{1,0:T(8,128)} %get-tuple-element.184, f32[36,256]{1,0:T(8,128)S(1)} %bitcast.197, ...), kind=kOutput, calls=%fused_computation.23.clone.1 | convolution fusion | flops 193757184 | bytes 2101392 | tf_op jit(solution)/shard_map/while/body/eval_jaxpr/nbs,bst->nbt/dot_general | solution.py:114
  467.0 14.8 %fusion.97 = f32[36,32,256]{2,1,0:T(8,128)S(1)} fusion(f32[36,256]{1,0:T(8,128)S(1)} %bitcast.194, f32[36,256]{1,0:T(8,128)} %get-tuple-element.181, f32[36,256]{1,0:T(8,128)S(1)} %bitcast.195, f32[36,256]{1,0:T(8,128)S(1)} %bitcast.196, f32[36,256]{1,0:T(8,128)} %get-tuple-element.184, f32[36,256]{1,0:T(8,128)S(1)} %bitcast.197, ...), kind=kOutput, calls=%fused_computation.23.clone.1 | convolution fusion | flops 193757184 | bytes 2101392 | tf_op jit(solution)/shard_map/while/body/eval_jaxpr/nbs,bst->nbt/dot_general | solution.py:114
  499.2 14.8 %fusion.97 = f32[36,32,256]{2,1,0:T(8,128)S(1)} fusion(f32[36,256]{1,0:T(8,128)S(1)} %bitcast.194, f32[36,256]{1,0:T(8,128)} %get-tuple-element.181, f32[36,256]{1,0:T(8,128)S(1)} %bitcast.195, f32[36,256]{1,0:T(8,128)S(1)} %bitcast.196, f32[36,256]{1,0:T(8,128)} %get-tuple-element.184, f32[36,256]{1,0:T(8,128)S(1)} %bitcast.197, ...), kind=kOutput, calls=%fused_computation.23.clone.1 | convolution fusion | flops 193757184 | bytes 2101392 | tf_op jit(solution)/shard_map/while/body/eval_jaxpr/nbs,bst->nbt/dot_general | solution.py:114
  531.5 14.8 %fusion.97 = f32[36,32,256]{2,1,0:T(8,128)S(1)} fusion(f32[36,256]{1,0:T(8,128)S(1)} %bitcast.194, f32[36,256]{1,0:T(8,128)} %get-tuple-element.181, f32[36,256]{1,0:T(8,128)S(1)} %bitcast.195, f32[36,256]{1,0:T(8,128)S(1)} %bitcast.196, f32[36,256]{1,0:T(8,128)} %get-tuple-element.184, f32[36,256]{1,0:T(8,128)S(1)} %bitcast.197, ...), kind=kOutput, calls=%fused_computation.23.clone.1 | convolution fusion | flops 193757184 | bytes 2101392 | tf_op jit(solution)/shard_map/while/body/eval_jaxpr/nbs,bst->nbt/dot_general | solution.py:114
  563.8 14.8 %fusion.97 = f32[36,32,256]{2,1,0:T(8,128)S(1)} fusion(f32[36,256]{1,0:T(8,128)S(1)} %bitcast.194, f32[36,256]{1,0:T(8,128)} %get-tuple-element.181, f32[36,256]{1,0:T(8,128)S(1)} %bitcast.195, f32[36,256]{1,0:T(8,128)S(1)} %bitcast.196, f32[36,256]{1,0:T(8,128)} %get-tuple-element.184, f32[36,256]{1,0:T(8,128)S(1)} %bitcast.197, ...), kind=kOutput, calls=%fused_computation.23.clone.1 | convolution fusion | flops 193757184 | bytes 2101392 | tf_op jit(solution)/shard_map/while/body/eval_jaxpr/nbs,bst->nbt/dot_general | solution.py:114
  596.0 14.8 %fusion.97 = f32[36,32,256]{2,1,0:T(8,128)S(1)} fusion(f32[36,256]{1,0:T(8,128)S(1)} %bitcast.194, f32[36,256]{1,0:T(8,128)} %get-tuple-element.181, f32[36,256]{1,0:T(8,128)S(1)} %bitcast.195, f32[36,256]{1,0:T(8,128)S(1)} %bitcast.196, f32[36,256]{1,0:T(8,128)} %get-tuple-element.184, f32[36,256]{1,0:T(8,128)S(1)} %bitcast.197, ...), kind=kOutput, calls=%fused_computation.23.clone.1 | convolution fusion | flops 193757184 | bytes 2101392 | tf_op jit(solution)/shard_map/while/body/eval_jaxpr/nbs,bst->nbt/dot_general | solution.py:114
  610.7 7.8 %scatter_fusion = f32[32,64,256]{2,0,1:T(8,128)} fusion(f32[32,64,256]{2,0,1:T(8,128)} %get-tuple-element.201, s32[36]{0:T(128)S(1)} %bitcast.204, f32[36,32,256]{2,1,0:T(8,128)S(1)} %fusion.97), kind=kCustom, calls=%fused_computation.7.clone.1 | custom fusion | flops 294912 | bytes 3539088 | tf_op jit(solution)/shard_map/while/body/eval_jaxpr/scatter-add | solution.py:118
  628.6 14.8 %fusion.97 = f32[36,32,256]{2,1,0:T(8,128)S(1)} fusion(f32[36,256]{1,0:T(8,128)S(1)} %bitcast.194, f32[36,256]{1,0:T(8,128)} %get-tuple-element.181, f32[36,256]{1,0:T(8,128)S(1)} %bitcast.195, f32[36,256]{1,0:T(8,128)S(1)} %bitcast.196, f32[36,256]{1,0:T(8,128)} %get-tuple-element.184, f32[36,256]{1,0:T(8,128)S(1)} %bitcast.197, ...), kind=kOutput, calls=%fused_computation.23.clone.1 | convolution fusion | flops 193757184 | bytes 2101392 | tf_op jit(solution)/shard_map/while/body/eval_jaxpr/nbs,bst->nbt/dot_general | solution.py:114
  660.9 14.8 %fusion.97 = f32[36,32,256]{2,1,0:T(8,128)S(1)} fusion(f32[36,256]{1,0:T(8,128)S(1)} %bitcast.194, f32[36,256]{1,0:T(8,128)} %get-tuple-element.181, f32[36,256]{1,0:T(8,128)S(1)} %bitcast.195, f32[36,256]{1,0:T(8,128)S(1)} %bitcast.196, f32[36,256]{1,0:T(8,128)} %get-tuple-element.184, f32[36,256]{1,0:T(8,128)S(1)} %bitcast.197, ...), kind=kOutput, calls=%fused_computation.23.clone.1 | convolution fusion | flops 193757184 | bytes 2101392 | tf_op jit(solution)/shard_map/while/body/eval_jaxpr/nbs,bst->nbt/dot_general | solution.py:114
  693.1 14.8 %fusion.97 = f32[36,32,256]{2,1,0:T(8,128)S(1)} fusion(f32[36,256]{1,0:T(8,128)S(1)} %bitcast.194, f32[36,256]{1,0:T(8,128)} %get-tuple-element.181, f32[36,256]{1,0:T(8,128)S(1)} %bitcast.195, f32[36,256]{1,0:T(8,128)S(1)} %bitcast.196, f32[36,256]{1,0:T(8,128)} %get-tuple-element.184, f32[36,256]{1,0:T(8,128)S(1)} %bitcast.197, ...), kind=kOutput, calls=%fused_computation.23.clone.1 | convolution fusion | flops 193757184 | bytes 2101392 | tf_op jit(solution)/shard_map/while/body/eval_jaxpr/nbs,bst->nbt/dot_general | solution.py:114
  (361 shorter events, 355.0 us)
Async XLA Ops:
  0.0 8.2 %copy-start = (bf16[64,64,256]{2,1,0:T(8,128)(2,1)S(1)}, bf16[64,64,256]{2,1,0:T(8,128)(2,1)}, u32[]{:S(2)}) copy-start(bf16[64,64,256]{2,1,0:T(8,128)(2,1)} %param.18) | copy-start | bytes 6291460
  0.0 20.7 %copy-start.1 = (bf16[32,16384]{1,0:T(8,128)(2,1)S(1)}, bf16[32,16384]{1,0:T(8,128)(2,1)}, u32[]{:S(2)}) copy-start(bf16[32,16384]{1,0:T(8,128)(2,1)} %param.13) | copy-start | bytes 3145732
  1.2 138.1 %copy-start.3 = (f32[6,8,8,256]{3,2,0,1:T(8,128)}, f32[6,8,8,256]{3,2,0,1:T(8,128)S(1)}, u32[]{:S(2)}) copy-start(f32[6,8,8,256]{3,2,0,1:T(8,128)S(1)} %copy.55) | copy-start | bytes 1179652
  4.5 17.8 %copy-start.9 = (s32[64,16]{0,1:T(8,128)S(1)}, s32[64,16]{0,1:T(8,128)}, u32[]{:S(2)}) copy-start(s32[64,16]{0,1:T(8,128)} %param.17) | copy-start | bytes 12292
  6.2 133.1 %collective-permute-start = (f32[64,1728]{1,0:T(8,128)}, f32[64,1728]{1,0:T(8,128)}, u32[]{:S(2)}, u32[]{:S(2)}) collective-permute-start(f32[64,1728]{1,0:T(8,128)} %pad_maximum_fusion.3), channel_id=1, source_target_pairs={{0,1},{1,2},{2,3},{3,4},{4,5},{5,6},{6,7},{7,8},{8,9},{9,10},{10,1... | collective-permute-start | bytes 1327112 | tf_op jit(solution)/shard_map/ppermute | solution.py:18
  7.8 131.5 %collective-permute-start.1 = (f32[64,1728]{1,0:T(8,128)}, f32[64,1728]{1,0:T(8,128)}, u32[]{:S(2)}, u32[]{:S(2)}) collective-permute-start(f32[64,1728]{1,0:T(8,128)} %pad_maximum_fusion.3), channel_id=1, source_target_pairs={{1,0},{2,1},{3,2},{4,3},{5,4},{6,5},{7,6},{8,7},{9,8},{10,9},{11,1... | collective-permute-start | bytes 1327112 | tf_op jit(solution)/shard_map/ppermute | solution.py:21
  10.1 0.8 copy-start.2
  14.2 96.9 %collective-permute-start.4 = (bf16[32,4096]{1,0:T(8,128)(2,1)}, bf16[32,4096]{1,0:T(8,128)(2,1)}, u32[]{:S(2)}, u32[]{:S(2)}) collective-permute-start(bf16[32,4096]{1,0:T(8,128)(2,1)} %reshape.193), channel_id=1, source_target_pairs={{0,1},{1,2},{2,3},{3,4},{4,5},{5,6},{6,7},{7,8},{8,9},{9,10},{10,1... | collective-permute-start | bytes 786440 | tf_op jit(solution)/shard_map/ppermute | solution.py:18
  15.7 105.9 %collective-permute-start.5 = (bf16[32,4096]{1,0:T(8,128)(2,1)}, bf16[32,4096]{1,0:T(8,128)(2,1)}, u32[]{:S(2)}, u32[]{:S(2)}) collective-permute-start(bf16[32,4096]{1,0:T(8,128)(2,1)} %reshape.193), channel_id=1, source_target_pairs={{1,0},{2,1},{3,2},{4,3},{5,4},{6,5},{7,6},{8,7},{9,8},{10,9},{11,1... | collective-permute-start | bytes 786440 | tf_op jit(solution)/shard_map/ppermute | solution.py:21
  21.8 172.5 %collective-permute-start.2 = (bf16[32,8192]{1,0:T(8,128)(2,1)}, bf16[32,8192]{1,0:T(8,128)(2,1)}, u32[]{:S(2)}, u32[]{:S(2)}) collective-permute-start(bf16[32,8192]{1,0:T(8,128)(2,1)} %get-tuple-element.96), channel_id=1, source_target_pairs={{0,1},{1,2},{2,3},{3,4},{4,5},{5,6},{6,7},{7,8},{8,9},{9,10},{10,1... | collective-permute-start | bytes 1572872 | tf_op jit(solution)/shard_map/ppermute | solution.py:18
  21.8 0.6 copy-start.10
  21.8 0.6 copy-start.11
  111.1 83.2 %collective-permute-start.3 = (bf16[32,8192]{1,0:T(8,128)(2,1)}, bf16[32,8192]{1,0:T(8,128)(2,1)}, u32[]{:S(2)}, u32[]{:S(2)}) collective-permute-start(bf16[32,8192]{1,0:T(8,128)(2,1)} %get-tuple-element.97), channel_id=1, source_target_pairs={{1,0},{2,1},{3,2},{4,3},{5,4},{6,5},{7,6},{8,7},{9,8},{10,9},{11,1... | collective-permute-start | bytes 1572872 | tf_op jit(solution)/shard_map/ppermute | solution.py:21
  151.7 1.8 copy-start.6
  151.7 1.8 copy-start.7
  151.7 1.8 copy-start.8
  153.6 35.6 %copy-start.4 = (f32[6,8,8,256]{3,2,0,1:T(8,128)S(1)}, f32[6,8,8,256]{3,2,0,1:T(8,128)}, u32[]{:S(2)}) copy-start(f32[6,8,8,256]{3,2,0,1:T(8,128)} %copy-done.3) | copy-start | bytes 1179652
  153.6 35.6 %copy-start.5 = (f32[64,192]{1,0:T(8,128)S(1)}, f32[64,192]{1,0:T(8,128)}, u32[]{:S(2)}) copy-start(f32[64,192]{1,0:T(8,128)} %copy.35) | copy-start | bytes 147460
where the time goes:
time: 737 us; the launch traced here: 724 us
  matrix products  285 us (39%)
  local copies, waits for them, and re-layouts  208 us (28%)
  other arithmetic  154 us (21%)
  blocking collectives  61.5 us (8%)
  starting transfers between devices  14.7 us (2%)
    dot_general x16, matrix products, near_step(): jnp.einsum('nbs,bst->nbt', source_density, kernel, preferred_element_type...  236 us
    scatter-add x16, other arithmetic, near_step(): return (totals.at[:, block_targets].add(partial_value), None)  120 us
    gather x16, local copies, waits for them, and re-layouts, near_step(): source_density = density_all[:, block_den]  48.4 us
    psum x1, blocking collectives, per_device(): group_total = lax.psum(partial_top, 'sub').astype(jnp.bfloat16)  40.7 us
    dot_general x1, matrix products, per_device(): jnp.einsum('nlfs,lfst->nlt', coeff_all[:, far_sources], far_kernel, prefe...  35.6 us
    gather x16, local copies, waits for them, and re-layouts, near_step(): target_pos = geometry[block_targets, :3]  32.2 us
    gather x16, local copies, waits for them, and re-layouts, near_step(): source_geo = source_geometry[block_geo]  31.7 us
    all_gather x1, blocking collectives, per_device(): coupled = lax.all_gather(group_total[None], 'leaf', axis=0, tiled=True)  20.7 us
  transfers between devices with their start and end apart: 6, of which 0 were waited for; matrix products, arithmetic and copies ran while one was open for 15% of the time, Pallas kernels for 0%

commit v1 on v0

v1 whole, which is shorter than its diff:
```python
import functools
import math

import jax
import jax.numpy as jnp
from jax import lax
from jax.experimental import pallas as pl
from jax.experimental.pallas import tpu as pltpu
from jax.sharding import PartitionSpec as P

SOFTEN = 0.01
FOUR_PI = 4.0 * math.pi
AXES = ("leaf", "sub")
LANES = 128
CHUNK = 32
SMEM = pl.BlockSpec(memory_space=pltpu.SMEM)
VMEM = pl.BlockSpec(memory_space=pltpu.VMEM)
PARAMS = pltpu.CompilerParams(vmem_limit_bytes=48 * 1024 * 1024)


def product(left, right, left_dim=1, right_dim=0):
    return lax.dot_general(
        left, right, (((left_dim,), (right_dim,)), ((), ())), preferred_element_type=jnp.float32
    )


def local(leaf, first, total):
    return lax.rem(leaf - first + (total + total // 2), total) - total // 2


def lift_kernel(density, bases, leaf_transfer, parent_transfer, coefficients, partial):
    parents = parent_transfer.shape[0]
    width = bases.shape[2]
    fan = bases.shape[0] // parents
    partial[...] = jnp.zeros_like(partial)

    def one_parent(p, _):
        lifted = jnp.zeros(partial.shape, jnp.float32)
        held = None
        for c in range(fan):
            l = p * fan + c
            start = pl.multiple_of(l * width, width)
            value = product(density[:, pl.ds(start, width)], bases[l], 1, 1).astype(jnp.bfloat16)
            lifted = lifted + product(value, leaf_transfer[l])
            if c % 2 == 0:
                held = value
            else:
                coefficients[p * (fan // 2) + c // 2] = jnp.concatenate([held, value], axis=1)
        partial[...] += product(lifted.astype(jnp.bfloat16), parent_transfer[p])
        return 0

    lax.fori_loop(0, parents, one_parent, 0)


def lift(density, bases, leaf_transfer, parent_transfer):
    leaves, rank, _ = bases.shape
    sides = density.shape[0]
    return pl.pallas_call(
        lift_kernel,
        out_shape=(
            jax.ShapeDtypeStruct((leaves // 2, sides, 2 * rank), jnp.bfloat16),
            jax.ShapeDtypeStruct((sides, rank), jnp.float32),
        ),
        in_specs=[VMEM] * 4,
        out_specs=(VMEM, VMEM),
        compiler_params=PARAMS,
    )(density, bases, leaf_transfer, parent_transfer)


def split(value):
    high = value.astype(jnp.bfloat16).astype(jnp.float32)
    left = value - high
    middle = left.astype(jnp.bfloat16).astype(jnp.float32)
    return high, middle, left - middle


def near_kernel(
    total, place, near_list, near_count, geo_own, geo_low, geo_high, den_own, den_low, den_high,
    near, task_target, task_source, source, target, density, lhs, column, flux, block,
):
    leaves = geo_own.shape[1]
    width = geo_own.shape[2]
    reach = geo_low.shape[1]
    everything = leaves + 2 * reach
    slots = near_list.shape[0]
    first = place[0]

    def put(ref, row, value):
        for b in range(0, width, LANES):
            ref[b // LANES, pl.ds(row, 8, stride=8), :] = value[:, b : b + LANES]

    def get(ref, row, count):
        return jnp.concatenate(
            [ref[b, pl.ds(row, count), :] for b in range(width // LANES)], axis=1
        )

    def append(t, position):
        live = near_count[t]
        for k in range(slots):
            s = local(near_list[k, t], first + t, total) + t
            s = jnp.where(s >= leaves, s + reach, jnp.where(s < 0, s + leaves + reach, s))
            task_source[position] = s
            task_target[position // 2] = t
            position = position + jnp.where(k < live, 1, 0)
        task_source[position] = everything
        return (position + 1) // 2 * 2

    for i in range(2):
        task_target[i] = leaves
        task_source[2 * i] = everything
        task_source[2 * i + 1] = everything
    ended = lax.fori_loop(0, leaves, append, 4)
    pairs = ended // 2 - 2
    for i in range(2):
        task_target[pairs + 2 + i] = leaves
        task_source[ended + 2 * i] = everything
        task_source[ended + 2 * i + 1] = everything

    center = [jnp.mean(geo_own[c], keepdims=True) for c in range(3)]
    for base, ref in ((0, geo_own), (leaves, geo_low), (leaves + reach, geo_high)):
        for g in range(0, ref.shape[1], 8):
            position = [ref[c, g : g + 8, :] for c in range(3)]
            normal = [ref[3 + c, g : g + 8, :] * (1.0 / FOUR_PI) for c in range(3)]
            moved = [value - middle for value, middle in zip(position, center)]
            shift = normal[0] * moved[0] + normal[1] * moved[1] + normal[2] * moved[2]
            row = (base + g) * 8
            for c in range(3):
                put(source, row + c, normal[c])
                put(source, row + 4 + c, position[c])
            put(source, row + 3, shift)
            put(source, row + 7, jnp.zeros_like(shift))
            if base == 0:
                for c in range(3):
                    put(target, row + c, moved[c])
                    put(target, row + 4 + c, position[c])
                put(target, row + 3, jnp.full_like(shift, -1.0))
                put(target, row + 7, jnp.zeros_like(shift))
        dens = {0: den_own, leaves: den_low, leaves + reach: den_high}[base]
        for l in range(ref.shape[1]):
            density[base + l] = dens[:, l * width : (l + 1) * width]
    density[everything] = jnp.zeros(density.shape[1:], density.dtype)
    for b in range(width // LANES):
        source[b, everything * 8 :, :] = jnp.zeros((8, LANES), jnp.float32)

    rows = lax.broadcasted_iota(jnp.int32, (8, width), 0)
    with_shift = (rows < 4).astype(jnp.float32)
    without = (rows < 3).astype(jnp.float32)

    def prepare(t, _):
        raw = get(target, pl.multiple_of(t * 8, 8), 8)
        high, middle, low = split(raw)
        led = high * with_shift
        second = middle * without
        stacked = jnp.concatenate([led, second, low * without, led, second, led, raw], axis=0)
        turned = stacked.T
        lhs[t] = turned[:, :48].astype(jnp.bfloat16)
        column[t] = turned[:, 48:]
        near[t] = jnp.zeros(near.shape[1:], near.dtype)
        return 0

    lax.fori_loop(0, leaves, prepare, 0)
    near[leaves] = jnp.zeros(near.shape[1:], near.dtype)
    block[...] = jnp.zeros_like(block)
    flux[...] = jnp.zeros_like(flux)

    def weights(s):
        high, middle, low = split(get(source, pl.multiple_of(s * 8, 8), 8))
        return jnp.concatenate([high, high, high, middle, middle, low], axis=0).astype(jnp.bfloat16)

    def step(j, _):
        t = task_target[j]
        both = jnp.concatenate([density[task_source[2 * j + i]] for i in range(2)], axis=1)
        near[t] += product(both, block[...], 1, 1)

        t = jnp.minimum(task_target[j + 1], leaves - 1)
        pair = [task_source[2 * j + 2 + i] for i in range(2)]
        places = [
            jnp.concatenate([get(source, s * 8 + 4 + a, 1) for s in pair], axis=1)
            for a in range(3)
        ]
        for r in range(0, width, CHUNK):
            lines = column[t, r : r + CHUNK, :]
            spread = [
                jnp.broadcast_to(lines[:, 4 + a : 5 + a], (CHUNK, LANES)) for a in range(3)
            ]
            for b in range(0, 2 * width, LANES):
                gap = [spread[a] - places[a][:, b : b + LANES] for a in range(3)]
                squared = gap[0] * gap[0] + gap[1] * gap[1] + (gap[2] * gap[2] + SOFTEN)
                inverse = lax.rsqrt(squared)
                value = flux[r : r + CHUNK, b : b + LANES] * inverse * (inverse * inverse)
                block[r : r + CHUNK, b : b + LANES] = value.astype(jnp.bfloat16)

        t = jnp.minimum(task_target[j + 2], leaves - 1)
        pair = [task_source[2 * j + 4 + i] for i in range(2)]
        flux[...] = product(lhs[t], jnp.concatenate([weights(s) for s in pair], axis=1))
        return 0

    lax.fori_loop(0, pairs + 2, step, 0)


def near_field(total, place, near_list, near_count, geometries, densities):
    leaves, width = geometries[0].shape[1:]
    everything = leaves + 2 * geometries[1].shape[1]
    sides = densities[0].shape[0]
    slots = near_list.shape[0]
    most = leaves * (slots // 2 + 1) + 8
    return pl.pallas_call(
        functools.partial(near_kernel, total),
        out_shape=jax.ShapeDtypeStruct((leaves + 1, sides, width), jnp.float32),
        in_specs=[SMEM] * 3 + [VMEM] * 6,
        out_specs=VMEM,
        scratch_shapes=[
            pltpu.SMEM((most,), jnp.int32),
            pltpu.SMEM((2 * most,), jnp.int32),
            pltpu.VMEM((width // LANES, (everything + 1) * 8, LANES), jnp.float32),
            pltpu.VMEM((width // LANES, leaves * 8, LANES), jnp.float32),
            pltpu.VMEM((everything + 1, sides, width), jnp.bfloat16),
            pltpu.VMEM((leaves, width, 48), jnp.bfloat16),
            pltpu.VMEM((leaves, width, 8), jnp.float32),
            pltpu.VMEM((width, 2 * width), jnp.float32),
            pltpu.VMEM((width, 2 * width), jnp.bfloat16),
        ],
        compiler_params=PARAMS,
    )(place, near_list, near_count, *geometries, *densities)


def final_kernel(
    total, place, far_list, top_far, top_proxies, coupled, coef_own, coef_low, coef_high,
    prox_own, prox_low, prox_high, near, density, bases, leaf_transfer, parent_transfer,
    out, charges, points, lines, parent_local,
):
    leaves, rank, width = bases.shape
    first = place[0]
    group = place[1]
    parents = parent_transfer.shape[0]
    fan = leaves // parents
    sides = density.shape[0]
    left = lax.broadcasted_iota(jnp.int32, (sides, LANES), 1) < rank
    row_left = lax.broadcasted_iota(jnp.int32, (1, LANES), 1) < rank

    def duplicate(value):
        return jnp.concatenate([value, value], axis=1)

    top_local = jnp.zeros((sides, rank), jnp.float32)
    stacked = jnp.concatenate(
        [top_proxies[c, pl.ds(group, 1), :] for c in range(3)]
        + [jnp.zeros((5, rank), jnp.float32)], axis=0,
    )
    turned = duplicate(stacked).T[:rank]
    for k in range(top_far.shape[0]):
        node = top_far[k, group]
        squared = jnp.full((rank, rank), SOFTEN, jnp.float32)
        for c in range(3):
            gap = turned[:, c : c + 1] - top_proxies[c, pl.ds(node, 1), :]
            squared = squared + gap * gap
        coupling = (lax.rsqrt(squared) * (1.0 / FOUR_PI)).astype(jnp.bfloat16)
        top_local = top_local + product(coupled[group ^ node], coupling, 1, 1)
    top_local = top_local.astype(jnp.bfloat16)
    for p in range(parents):
        parent_local[p] = product(top_local, parent_transfer[p], 1, 1).astype(jnp.bfloat16)

    for base, ref, prox in (
        (0, coef_low, prox_low), (leaves, coef_own, prox_own), (2 * leaves, coef_high, prox_high)
    ):
        for i in range(leaves // 2):
            value = ref[i].astype(jnp.float32)
            turned = pltpu.roll(value, rank, 1)
            charges[base + 2 * i] = jnp.where(left, value, turned).astype(jnp.bfloat16)
            charges[base + 2 * i + 1] = jnp.where(left, turned, value).astype(jnp.bfloat16)
        for c in range(3):
            points[c, base : base + leaves, :] = duplicate(prox[c])
    for g in range(0, leaves, 8):
        for c in range(3):
            lines[pl.ds(g * 8 + c, 8, stride=8), :] = points[c, leaves + g : leaves + g + 8, :]
        for c in range(3, 8):
            lines[pl.ds(g * 8 + c, 8, stride=8), :] = jnp.zeros((8, LANES), jnp.float32)

    def one_leaf(t):
        turned = lines[pl.ds(pl.multiple_of(t * 8, 8), 8), :].T[:rank]
        spread = [jnp.broadcast_to(turned[:, c : c + 1], (rank, LANES)) for c in range(3)]
        blocks = []
        values = []
        for q in range(far_list.shape[0] // 2):
            pair = [
                local(far_list[2 * q + i, t], first + t, total) + t + leaves for i in range(2)
            ]
            gap = [
                spread[c]
                - jnp.where(
                    row_left, points[c, pl.ds(pair[0], 1), :], points[c, pl.ds(pair[1], 1), :]
                )
                for c in range(3)
            ]
            squared = gap[0] * gap[0] + gap[1] * gap[1] + (gap[2] * gap[2] + SOFTEN)
            blocks.append((lax.rsqrt(squared) * (1.0 / FOUR_PI)).astype(jnp.bfloat16))
            values.append(jnp.where(left, charges[pair[0]], charges[pair[1]]))
        far = product(jnp.concatenate(values, axis=1), jnp.concatenate(blocks, axis=1), 1, 1)
        leaf_local = far + product(parent_local[t // fan], leaf_transfer[t], 1, 1)
        start = pl.multiple_of(t * width, width)
        result = 0.5 * density[:, pl.ds(start, width)].astype(jnp.float32) + near[t]
        out[:, pl.ds(start, width)] = result + product(leaf_local.astype(jnp.bfloat16), bases[t])

    def some(j, _):
        for i in range(2):
            one_leaf(2 * j + i)
        return 0

    lax.fori_loop(0, leaves // 2, some, 0)


def finish(total, place, far_list, top_far, top_proxies, coupled, coefs, proxies, near, density,
           bases, leaf_transfer, parent_transfer):
    leaves, rank, width = bases.shape
    sides = density.shape[0]
    return pl.pallas_call(
        functools.partial(final_kernel, total),
        out_shape=jax.ShapeDtypeStruct(density.shape, jnp.float32),
        in_specs=[SMEM] * 3 + [VMEM] * 13,
        out_specs=VMEM,
        scratch_shapes=[
            pltpu.VMEM((3 * leaves, sides, LANES), jnp.bfloat16),
            pltpu.VMEM((3, 3 * leaves, LANES), jnp.float32),
            pltpu.VMEM((leaves * 8, LANES), jnp.float32),
            pltpu.VMEM((parent_transfer.shape[0], sides, rank), jnp.bfloat16),
        ],
        compiler_params=PARAMS,
    )(place, far_list, top_far, top_proxies, coupled, *coefs, *proxies, near, density, bases,
      leaf_transfer, parent_transfer)


def per_device(
    density, geometry, near_list, near_count, far_list, bases, proxies, leaf_transfer,
    parent_transfer, top_proxies, top_far,
):
    leaves, _, width = geometry.shape
    devices = lax.axis_size(AXES)
    total = leaves * devices
    group = lax.axis_index("leaf")
    place = jnp.stack([lax.axis_index(AXES) * leaves, group]).astype(jnp.int32)
    reach = leaves // 2
    forward = [(i, (i + 1) % devices) for i in range(devices)]
    backward = [(b, a) for a, b in forward]
    geometry = jnp.transpose(geometry, (1, 0, 2))
    proxies = jnp.transpose(proxies, (1, 0, 2))
    near_list = jnp.transpose(near_list)
    far_list = jnp.transpose(far_list)
    top_proxies = jnp.transpose(top_proxies, (1, 0, 2))
    top_far = jnp.transpose(top_far)

    geo_low = lax.ppermute(geometry[:, leaves - reach :], AXES, forward)
    geo_high = lax.ppermute(geometry[:, :reach], AXES, backward)
    den_low = lax.ppermute(density[:, (leaves - reach) * width :], AXES, forward)
    den_high = lax.ppermute(density[:, : reach * width], AXES, backward)
    prox_low = lax.ppermute(proxies, AXES, forward)
    prox_high = lax.ppermute(proxies, AXES, backward)

    coefficients, partial = lift(density, bases, leaf_transfer, parent_transfer)
    coef_low = lax.ppermute(coefficients, AXES, forward)
    coef_high = lax.ppermute(coefficients, AXES, backward)

    count = lax.axis_size("sub")
    step = 1
    while step < count:
        partial = partial + lax.ppermute(partial, "sub", [(i, i ^ step) for i in range(count)])
        step *= 2
    coupled = partial.astype(jnp.bfloat16)[None]
    count = lax.axis_size("leaf")
    step = 1
    while step < count:
        other = lax.ppermute(coupled, "leaf", [(i, i ^ step) for i in range(count)])
        coupled = jnp.concatenate([coupled, other], axis=0)
        step *= 2

    near = near_field(
        total, place, near_list, near_count,
        (geometry, geo_low, geo_high), (density, den_low, den_high),
    )
    return finish(
        total, place, far_list, top_far, top_proxies, coupled,
        (coefficients, coef_low, coef_high), (proxies, prox_low, prox_high),
        near, density, bases, leaf_transfer, parent_transfer,
    )


def solution(mesh):
    placed = (
        P(None, AXES),
        P(AXES, None, None),
        P(AXES, None),
        P(AXES),
        P(AXES, None),
        P(AXES, None, None),
        P(AXES, None, None),
        P(AXES, None, None),
        P(AXES, None, None),
        P(),
        P(),
    )
    return jax.shard_map(
        per_device, mesh=mesh, in_specs=placed, out_specs=P(None, AXES), check_vma=False
    )
```

time: 737 us -> 188 us (0.26); the launches traced: 724 us -> 189 us
  matrix products: 285 us -> 0 us
  local copies, waits for them, and re-layouts: 208 us -> 8.22 us
  other arithmetic: 154 us -> 0.13 us
  Pallas kernels: 0 us -> 127 us
  blocking collectives: 61.5 us -> 0 us
  waiting for transfers between devices: 0.02 us -> 20.9 us
  starting transfers between devices: 14.7 us -> 33.4 us
    dot_general x22 -> x0, matrix products: 285 us -> none  [the longest x16 236 us: near_step(): jnp.einsum('nbs,bst->nbt', source_density, kernel, preferred_element_type...]
    gather x53 -> x0, local copies, waits for them, and re-layouts: 137 us -> none  [the longest x16 48.4 us: near_step(): source_density = density_all[:, block_den]]
    pallas_call x0 -> x3, Pallas kernels: none -> 127 us  [the longest x1 95.4 us: near_field(): pl.pallas_call(functools.partial(near_kernel, total), out_shape=jax.Shape...]
    scatter-add x16 -> x0, other arithmetic: 120 us -> none  [near_step(): return (totals.at[:, block_targets].add(partial_value), None)]
    psum x1 -> x0, blocking collectives: 40.7 us -> none  [per_device(): group_total = lax.psum(partial_top, 'sub').astype(jnp.bfloat16)]
    ppermute x6 -> x15, waiting for transfers between devices: 0.02 us -> 20.9 us  [the longest x3 8.09 us: per_device(): lax.ppermute(partial, 'sub', [(i, i ^ step) for i in range(count)])]
    all_gather x1 -> x0, blocking collectives: 20.7 us -> none  [per_device(): coupled = lax.all_gather(group_total[None], 'leaf', axis=0, tiled=True)]
    ppermute x6 -> x15, starting transfers between devices: 14.7 us -> 33.4 us  [the longest x1 8.8 us: per_device(): prox_high = lax.ppermute(proxies, AXES, backward)]
  transfers between devices with their start and end apart: 6 -> 15, of which waited for: 0 -> 6; matrix products, arithmetic and copies ran while one was open for 15% -> 1% of each run, Pallas kernels for 0% -> 50%
where the time goes in v1:
time: 188 us; the launch traced here: 189 us
  Pallas kernels  127 us (68%)
  starting transfers between devices  33.4 us (18%)
  waiting for transfers between devices  20.9 us (11%)
  local copies, waits for them, and re-layouts  8.22 us (4%)
    pallas_call x1, Pallas kernels, near_field(): pl.pallas_call(functools.partial(near_kernel, total), out_shape=jax.Shape...  95.4 us
    pallas_call x1, Pallas kernels, finish(): pl.pallas_call(functools.partial(final_kernel, total), out_shape=jax.Shap...  26.6 us
    ppermute x1, starting transfers between devices, per_device(): prox_high = lax.ppermute(proxies, AXES, backward)  8.8 us
    ppermute x3, waiting for transfers between devices, per_device(): lax.ppermute(partial, 'sub', [(i, i ^ step) for i in range(count)])  8.09 us
    ppermute x4, waiting for transfers between devices, per_device(): other = lax.ppermute(coupled, 'leaf', [(i, i ^ step) for i in range(count)])  7.26 us
    ppermute x1, starting transfers between devices, per_device(): geo_low = lax.ppermute(geometry[:, leaves - reach:], AXES, forward)  6.58 us
    unnamed x35, local copies, waits for them, and re-layouts  6.38 us
    ppermute x1, starting transfers between devices, per_device(): den_high = lax.ppermute(density[:, :reach * width], AXES, backward)  5.96 us
  transfers between devices with their start and end apart: 15, of which 6 were waited for; matrix products, arithmetic and copies ran while one was open for 1% of the time, Pallas kernels for 50%

profile of v1, /device:TPU:8, one launch (start us, length us, event | category | flops | bytes accessed | tf_op | source)
XLA Modules:
  0.0 189.5 jit_solution(11005379142159383478)
XLA Ops:
  0.0 1.2 copy-done
  1.2 1.6 copy-done.3
  2.8 1.2 copy-done.5
  4.0 0.9 copy-done.8
  4.9 4.6 %shard_map.109 = (bf16[32,32,128]{2,1,0:T(8,128)(2,1)S(1)}, f32[32,64]{1,0:T(8,128)S(1)}) custom-call(bf16[32,16384]{1,0:T(8,128)(2,1)S(1)} %copy-done, bf16[64,64,256]{2,1,0:T(8,128)(2,1)S(1)} %copy-done.3, bf16[64,64,64]{2,1,0:T(8,128)(2,1)S(1)} %copy-done.5, bf16[8,64,64]{2,1,0:T(8,128)(2,1)S(1)} %copy-done.8), custom_call_target="tpu_custom_call" | custom-call | tf_op jit(solution)/shard_map/pallas_call | solution.py:58
  10.0 3.4 %collective-permute-done = f32[32,64]{1,0:T(8,128)S(1)} collective-permute-done((f32[32,64]{1,0:T(8,128)S(1)}, f32[32,64]{1,0:T(8,128)S(1)}, u32[]{:S(2)}, u32[]{:S(2)}) %collective-permute-start) | collective-permute-done | bytes 8224 | tf_op jit(solution)/shard_map/ppermute | solution.py:364
  13.4 2.3 %collective-permute-start.1 = (f32[32,64]{1,0:T(8,128)S(1)}, f32[32,64]{1,0:T(8,128)S(1)}, u32[]{:S(2)}, u32[]{:S(2)}) collective-permute-start(f32[32,64]{1,0:T(8,128)S(1)} %add.13), channel_id=1, source_target_pairs={{0,2},{1,3},{2,0},{3,1},{4,6},{5,7},{6,4},{7,5},{8,10},{9,11},{10,... | collective-permute-start | bytes 24584 | tf_op jit(solution)/shard_map/ppermute | solution.py:364
  15.7 2.9 %collective-permute-done.1 = f32[32,64]{1,0:T(8,128)S(1)} collective-permute-done((f32[32,64]{1,0:T(8,128)S(1)}, f32[32,64]{1,0:T(8,128)S(1)}, u32[]{:S(2)}, u32[]{:S(2)}) %collective-permute-start.1) | collective-permute-done | bytes 8224 | tf_op jit(solution)/shard_map/ppermute | solution.py:364
  18.6 3.0 %collective-permute-start.2 = (f32[32,64]{1,0:T(8,128)S(1)}, f32[32,64]{1,0:T(8,128)S(1)}, u32[]{:S(2)}, u32[]{:S(2)}) collective-permute-start(f32[32,64]{1,0:T(8,128)S(1)} %add.14), channel_id=1, source_target_pairs={{0,4},{1,5},{2,6},{3,7},{4,0},{5,1},{6,2},{7,3},{8,12},{9,13},{10,... | collective-permute-start | bytes 24584 | tf_op jit(solution)/shard_map/ppermute | solution.py:364
  22.1 1.8 collective-permute-done.2
  23.9 0.8 fusion.3
  24.7 2.2 %collective-permute-start.12 = (f32[6,32,256]{2,1,0:T(8,128)}, f32[6,32,256]{2,1,0:T(8,128)S(1)}, u32[]{:S(2)}, u32[]{:S(2)}) collective-permute-start(f32[6,32,256]{2,1,0:T(8,128)} %get-tuple-element.13), channel_id=1, source_target_pairs={{1,0},{2,1},{3,2},{4,3},{5,4},{6,5},{7,6},{8,7},{9,8},{10,9},{11,1... | collective-permute-start | bytes 589832 | tf_op jit(solution)/shard_map/ppermute | solution.py:351
  26.9 1.1 collective-permute-start.4
  28.1 1.0 fusion.2
  29.1 6.0 %collective-permute-start.14 = (bf16[32,8192]{1,0:T(8,128)(2,1)}, bf16[32,8192]{1,0:T(8,128)(2,1)S(1)}, u32[]{:S(2)}, u32[]{:S(2)}) collective-permute-start(bf16[32,8192]{1,0:T(8,128)(2,1)} %get-tuple-element.11), channel_id=1, source_target_pairs={{1,0},{2,1},{3,2},{4,3},{5,4},{6,5},{7,6},{8,7},{9,8},{10,9},{11,1... | collective-permute-start | bytes 1572872 | tf_op jit(solution)/shard_map/ppermute | solution.py:353
  35.1 2.2 %collective-permute-start.5 = (bf16[4,32,64]{2,1,0:T(8,128)(2,1)S(1)}, bf16[4,32,64]{2,1,0:T(8,128)(2,1)S(1)}, u32[]{:S(2)}, u32[]{:S(2)}) collective-permute-start(bf16[4,32,64]{2,1,0:T(8,128)(2,1)S(1)} %pad_maximum_fusion.1), channel_id=1, source_target_pairs={{0,32},{8,40},{16,48},{24,56},{32,0},{40,8},{48,16},{56,24},{64,96... | collective-permute-start | bytes 49160 | tf_op jit(solution)/shard_map/ppermute | solution.py:370
  37.4 3.2 %collective-permute-done.5 = bf16[4,32,64]{2,1,0:T(8,128)(2,1)S(1)} collective-permute-done((bf16[4,32,64]{2,1,0:T(8,128)(2,1)S(1)}, bf16[4,32,64]{2,1,0:T(8,128)(2,1)S(1)}, u32[]{:S(2)}, u32[]{:S(2)}) %collective-permute-start.5) | collective-permute-done | bytes 16416 | tf_op jit(solution)/shard_map/ppermute | solution.py:370
  40.9 4.0 %collective-permute-done.6 = bf16[8,32,64]{2,1,0:T(8,128)(2,1)S(1)} collective-permute-done((bf16[8,32,64]{2,1,0:T(8,128)(2,1)S(1)}, bf16[8,32,64]{2,1,0:T(8,128)(2,1)S(1)}, u32[]{:S(2)}, u32[]{:S(2)}) %collective-permute-start.6) | collective-permute-done | bytes 32800 | tf_op jit(solution)/shard_map/ppermute | solution.py:370
  45.0 6.6 %collective-permute-start.11 = (f32[6,32,256]{2,1,0:T(8,128)}, f32[6,32,256]{2,1,0:T(8,128)S(1)}, u32[]{:S(2)}, u32[]{:S(2)}) collective-permute-start(f32[6,32,256]{2,1,0:T(8,128)} %get-tuple-element.14), channel_id=1, source_target_pairs={{0,1},{1,2},{2,3},{3,4},{4,5},{5,6},{6,7},{7,8},{8,9},{9,10},{10,1... | collective-permute-start | bytes 589832 | tf_op jit(solution)/shard_map/ppermute | solution.py:350
  51.6 5.5 %collective-permute-done.11.geo_low = f32[6,32,256]{2,1,0:T(8,128)S(1)} collective-permute-done((f32[6,32,256]{2,1,0:T(8,128)}, f32[6,32,256]{2,1,0:T(8,128)S(1)}, u32[]{:S(2)}, u32[]{:S(2)}) %collective-permute-start.11) | collective-permute-done | bytes 196640 | tf_op jit(solution)/shard_map/ppermute | solution.py:350
  57.1 8.8 %collective-permute-start.10 = (f32[3,64,64]{2,1,0:T(8,128)S(1)}, f32[3,64,64]{2,1,0:T(8,128)S(1)}, u32[]{:S(2)}, u32[]{:S(2)}) collective-permute-start(f32[3,64,64]{2,1,0:T(8,128)S(1)} %bitcast.13), channel_id=1, source_target_pairs={{1,0},{2,1},{3,2},{4,3},{5,4},{6,5},{7,6},{8,7},{9,8},{10,9},{11,1... | collective-permute-start | bytes 147464 | tf_op jit(solution)/shard_map/ppermute | solution.py:355
  66.0 95.4 %shard_map.110.near = f32[65,32,256]{2,1,0:T(8,128)S(1)} custom-call(s32[2]{0:T(128)S(1)} %pad_add_fusion.place, s32[9,64]{1,0:T(8,128)S(1)} %bitcast.17, s32[64]{0:T(128)S(1)} %copy-done.15, f32[6,64,256]{2,1,0:T(8,128)S(1)} %bitcast.12, f32[6,32,256]{2,1,0:T(8,128)S(1)} %collective-permute-done.11.geo_low, ...), custom_call_target="tpu_custom_call" | custom-call | tf_op jit(solution)/shard_map/pallas_call | solution.py:207
  161.5 1.3 copy-done.2
  162.9 26.6 %shard_map.111 = f32[32,16384]{1,0:T(8,128)} custom-call(s32[2]{0:T(128)S(1)} %pad_add_fusion.place, s32[16,64]{1,0:T(8,128)S(1)} %bitcast.18, s32[8,16]{1,0:T(8,128)S(1)} %bitcast.19, f32[3,16,64]{2,1,0:T(8,128)S(1)} %bitcast.16, bf16[16,32,64]{2,1,0:T(8,128)(2,1)S(1)} %constant_dynamic-update-slice_fusion.coupled, ...), custom_call_target="tpu_custom_call" | custom-call | tf_op jit(solution)/shard_map/pallas_call | solution.py:315
  (54 shorter events, 1.5 us)
Async XLA Ops:
  9.5 56.4 %copy-start.1 = (bf16[32,16384]{1,0:T(8,128)(2,1)S(1)}, bf16[32,16384]{1,0:T(8,128)(2,1)}, u32[]{:S(2)}) copy-start(bf16[32,16384]{1,0:T(8,128)(2,1)} %density.3) | copy-start | bytes 3145732
  9.5 56.4 %copy-start.12 = (s32[64,9]{0,1:T(8,128)S(1)}, s32[64,9]{0,1:T(8,128)}, u32[]{:S(2)}) copy-start(s32[64,9]{0,1:T(8,128)} %param.13) | copy-start | bytes 6916
  9.5 56.4 %copy-start.15 = (s32[64]{0:T(128)S(1)}, s32[64]{0:T(128)}, u32[]{:S(2)}) copy-start(s32[64]{0:T(128)} %near_count.1) | copy-start | bytes 772
  9.6 3.8 %collective-permute-start = (f32[32,64]{1,0:T(8,128)S(1)}, f32[32,64]{1,0:T(8,128)S(1)}, u32[]{:S(2)}, u32[]{:S(2)}) collective-permute-start(f32[32,64]{1,0:T(8,128)S(1)} %get-tuple-element.7), channel_id=1, source_target_pairs={{0,1},{1,0},{2,3},{3,2},{4,5},{5,4},{6,7},{7,6},{8,9},{9,8},{10,11... | collective-permute-start | bytes 24584 | tf_op jit(solution)/shard_map/ppermute | solution.py:364
  13.4 5.2 %collective-permute-start.1 = (f32[32,64]{1,0:T(8,128)S(1)}, f32[32,64]{1,0:T(8,128)S(1)}, u32[]{:S(2)}, u32[]{:S(2)}) collective-permute-start(f32[32,64]{1,0:T(8,128)S(1)} %add.13), channel_id=1, source_target_pairs={{0,2},{1,3},{2,0},{3,1},{4,6},{5,7},{6,4},{7,5},{8,10},{9,11},{10,... | collective-permute-start | bytes 24584 | tf_op jit(solution)/shard_map/ppermute | solution.py:364
  18.6 5.2 %collective-permute-start.2 = (f32[32,64]{1,0:T(8,128)S(1)}, f32[32,64]{1,0:T(8,128)S(1)}, u32[]{:S(2)}, u32[]{:S(2)}) collective-permute-start(f32[32,64]{1,0:T(8,128)S(1)} %add.14), channel_id=1, source_target_pairs={{0,4},{1,5},{2,6},{3,7},{4,0},{5,1},{6,2},{7,3},{8,12},{9,13},{10,... | collective-permute-start | bytes 24584 | tf_op jit(solution)/shard_map/ppermute | solution.py:364
  21.6 141.2 %collective-permute-start.8 = (bf16[32,32,128]{2,1,0:T(8,128)(2,1)S(1)}, bf16[32,32,128]{2,1,0:T(8,128)(2,1)S(1)}, u32[]{:S(2)}, u32[]{:S(2)}) collective-permute-start(bf16[32,32,128]{2,1,0:T(8,128)(2,1)S(1)} %get-tuple-element.8.coef_own), channel_id=1, source_target_pairs={{1,0},{2,1},{3,2},{4,3},{5,4},{6,5},{7,6},{8,7},{9,8},{10,9},{11,1... | collective-permute-start | bytes 786440 | tf_op jit(solution)/shard_map/ppermute | solution.py:359
  23.9 3.1 %collective-permute-start.3 = (bf16[1,32,64]{2,1,0:T(8,128)(2,1)S(1)}, bf16[1,32,64]{2,1,0:T(8,128)(2,1)S(1)}, u32[]{:S(2)}, u32[]{:S(2)}) collective-permute-start(bf16[1,32,64]{2,1,0:T(8,128)(2,1)S(1)} %get-tuple-element.10), channel_id=1, source_target_pairs={{0,8},{8,0},{16,24},{24,16},{32,40},{40,32},{48,56},{56,48},{64,72... | collective-permute-start | bytes 12296 | tf_op jit(solution)/shard_map/ppermute | solution.py:370
  24.7 20.3 %collective-permute-start.12 = (f32[6,32,256]{2,1,0:T(8,128)}, f32[6,32,256]{2,1,0:T(8,128)S(1)}, u32[]{:S(2)}, u32[]{:S(2)}) collective-permute-start(f32[6,32,256]{2,1,0:T(8,128)} %get-tuple-element.13), channel_id=1, source_target_pairs={{1,0},{2,1},{3,2},{4,3},{5,4},{6,5},{7,6},{8,7},{9,8},{10,9},{11,1... | collective-permute-start | bytes 589832 | tf_op jit(solution)/shard_map/ppermute | solution.py:351
  26.9 8.1 %collective-permute-start.4 = (bf16[2,32,64]{2,1,0:T(8,128)(2,1)S(1)}, bf16[2,32,64]{2,1,0:T(8,128)(2,1)S(1)}, u32[]{:S(2)}, u32[]{:S(2)}) collective-permute-start(bf16[2,32,64]{2,1,0:T(8,128)(2,1)S(1)} %pad_maximum_fusion.2), channel_id=1, source_target_pairs={{0,16},{8,24},{16,0},{24,8},{32,48},{40,56},{48,32},{56,40},{64,80... | collective-permute-start | bytes 24584 | tf_op jit(solution)/shard_map/ppermute | solution.py:370
  29.1 36.8 %collective-permute-start.14 = (bf16[32,8192]{1,0:T(8,128)(2,1)}, bf16[32,8192]{1,0:T(8,128)(2,1)S(1)}, u32[]{:S(2)}, u32[]{:S(2)}) collective-permute-start(bf16[32,8192]{1,0:T(8,128)(2,1)} %get-tuple-element.11), channel_id=1, source_target_pairs={{1,0},{2,1},{3,2},{4,3},{5,4},{6,5},{7,6},{8,7},{9,8},{10,9},{11,1... | collective-permute-start | bytes 1572872 | tf_op jit(solution)/shard_map/ppermute | solution.py:353
  35.1 30.9 %collective-permute-start.13 = (bf16[32,8192]{1,0:T(8,128)(2,1)}, bf16[32,8192]{1,0:T(8,128)(2,1)S(1)}, u32[]{:S(2)}, u32[]{:S(2)}) collective-permute-start(bf16[32,8192]{1,0:T(8,128)(2,1)} %get-tuple-element.12), channel_id=1, source_target_pairs={{0,1},{1,2},{2,3},{3,4},{4,5},{5,6},{6,7},{7,8},{8,9},{9,10},{10,1... | collective-permute-start | bytes 1572872 | tf_op jit(solution)/shard_map/ppermute | solution.py:352
  35.1 5.5 %collective-permute-start.5 = (bf16[4,32,64]{2,1,0:T(8,128)(2,1)S(1)}, bf16[4,32,64]{2,1,0:T(8,128)(2,1)S(1)}, u32[]{:S(2)}, u32[]{:S(2)}) collective-permute-start(bf16[4,32,64]{2,1,0:T(8,128)(2,1)S(1)} %pad_maximum_fusion.1), channel_id=1, source_target_pairs={{0,32},{8,40},{16,48},{24,56},{32,0},{40,8},{48,16},{56,24},{64,96... | collective-permute-start | bytes 49160 | tf_op jit(solution)/shard_map/ppermute | solution.py:370
  40.6 4.3 %collective-permute-start.6 = (bf16[8,32,64]{2,1,0:T(8,128)(2,1)S(1)}, bf16[8,32,64]{2,1,0:T(8,128)(2,1)S(1)}, u32[]{:S(2)}, u32[]{:S(2)}) collective-permute-start(bf16[8,32,64]{2,1,0:T(8,128)(2,1)S(1)} %pad_maximum_fusion), channel_id=1, source_target_pairs={{0,64},{8,72},{16,80},{24,88},{32,96},{40,104},{48,112},{56,120},{... | collective-permute-start | bytes 98312 | tf_op jit(solution)/shard_map/ppermute | solution.py:370
  45.0 117.9 %collective-permute-start.7 = (bf16[32,32,128]{2,1,0:T(8,128)(2,1)S(1)}, bf16[32,32,128]{2,1,0:T(8,128)(2,1)S(1)}, u32[]{:S(2)}, u32[]{:S(2)}) collective-permute-start(bf16[32,32,128]{2,1,0:T(8,128)(2,1)S(1)} %get-tuple-element.8.coef_own), channel_id=1, source_target_pairs={{0,1},{1,2},{2,3},{3,4},{4,5},{5,6},{6,7},{7,8},{8,9},{9,10},{10,1... | collective-permute-start | bytes 786440 | tf_op jit(solution)/shard_map/ppermute | solution.py:358
  45.0 12.1 %collective-permute-start.11 = (f32[6,32,256]{2,1,0:T(8,128)}, f32[6,32,256]{2,1,0:T(8,128)S(1)}, u32[]{:S(2)}, u32[]{:S(2)}) collective-permute-start(f32[6,32,256]{2,1,0:T(8,128)} %get-tuple-element.14), channel_id=1, source_target_pairs={{0,1},{1,2},{2,3},{3,4},{4,5},{5,6},{6,7},{7,8},{8,9},{9,10},{10,1... | collective-permute-start | bytes 589832 | tf_op jit(solution)/shard_map/ppermute | solution.py:350
  57.1 105.7 %collective-permute-start.10 = (f32[3,64,64]{2,1,0:T(8,128)S(1)}, f32[3,64,64]{2,1,0:T(8,128)S(1)}, u32[]{:S(2)}, u32[]{:S(2)}) collective-permute-start(f32[3,64,64]{2,1,0:T(8,128)S(1)} %bitcast.13), channel_id=1, source_target_pairs={{1,0},{2,1},{3,2},{4,3},{5,4},{6,5},{7,6},{8,7},{9,8},{10,9},{11,1... | collective-permute-start | bytes 147464 | tf_op jit(solution)/shard_map/ppermute | solution.py:355
  65.9 96.9 %collective-permute-start.9 = (f32[3,64,64]{2,1,0:T(8,128)S(1)}, f32[3,64,64]{2,1,0:T(8,128)S(1)}, u32[]{:S(2)}, u32[]{:S(2)}) collective-permute-start(f32[3,64,64]{2,1,0:T(8,128)S(1)} %bitcast.14), channel_id=1, source_target_pairs={{0,1},{1,2},{2,3},{3,4},{4,5},{5,6},{6,7},{7,8},{8,9},{9,10},{10,1... | collective-permute-start | bytes 147464 | tf_op jit(solution)/shard_map/ppermute | solution.py:354
  66.0 96.9 %copy-start.4 = (bf16[64,64,256]{2,1,0:T(8,128)(2,1)S(1)}, bf16[64,64,256]{2,1,0:T(8,128)(2,1)}, u32[]{:S(2)}) copy-start(bf16[64,64,256]{2,1,0:T(8,128)(2,1)} %bases.3) | copy-start | bytes 6291460
  66.0 96.9 %copy-start.6 = (bf16[64,64,64]{2,1,0:T(8,128)(2,1)S(1)}, bf16[64,64,64]{2,1,0:T(8,128)(2,1)}, u32[]{:S(2)}) copy-start(bf16[64,64,64]{2,1,0:T(8,128)(2,1)} %leaf_transfer.3) | copy-start | bytes 1572868
  66.0 96.9 %copy-start.9 = (bf16[8,64,64]{2,1,0:T(8,128)(2,1)S(1)}, bf16[8,64,64]{2,1,0:T(8,128)(2,1)}, u32[]{:S(2)}) copy-start(bf16[8,64,64]{2,1,0:T(8,128)(2,1)} %parent_transfer.3) | copy-start | bytes 196612
  66.0 96.9 %copy-start.11 = (f32[16,3,64]{2,0,1:T(8,128)S(1)}, f32[16,3,64]{2,0,1:T(8,128)}, u32[]{:S(2)}) copy-start(f32[16,3,64]{2,0,1:T(8,128)} %param.20) | copy-start | bytes 36868
  66.0 96.9 %copy-start.13 = (s32[64,16]{0,1:T(8,128)S(1)}, s32[64,16]{0,1:T(8,128)}, u32[]{:S(2)}) copy-start(s32[64,16]{0,1:T(8,128)} %param.15) | copy-start | bytes 12292
  66.0 96.9 %copy-start.14 = (s32[16,8]{0,1:T(8,128)S(1)}, s32[16,8]{0,1:T(8,128)}, u32[]{:S(2)}) copy-start(s32[16,8]{0,1:T(8,128)} %param.21) | copy-start | bytes 1540
  (7 other events, 72.8 us)

commit v2 on v1

--- a/solution.py
+++ b/solution.py
@@ -12,7 +12,8 @@
 FOUR_PI = 4.0 * math.pi
 AXES = ("leaf", "sub")
 LANES = 128
-CHUNK = 32
+CHUNK = 16
+FAR_UNROLL = 8
 SMEM = pl.BlockSpec(memory_space=pltpu.SMEM)
 VMEM = pl.BlockSpec(memory_space=pltpu.VMEM)
 PARAMS = pltpu.CompilerParams(vmem_limit_bytes=48 * 1024 * 1024)
@@ -25,44 +26,51 @@
 
 
 def local(leaf, first, total):
-    return lax.rem(leaf - first + (total + total // 2), total) - total // 2
+    moved = leaf - first + (total + total // 2)
+    if total & (total - 1) == 0:
+        return (moved & (total - 1)) - total // 2
+    return lax.rem(moved, total) - total // 2
 
 
 def lift_kernel(density, bases, leaf_transfer, parent_transfer, coefficients, partial):
+    fan, _, width = bases.shape
+
+    @pl.when(pl.program_id(0) == 0)
+    def _():
+        partial[...] = jnp.zeros_like(partial)
+
+    values = [
+        product(density[:, c * width : (c + 1) * width], bases[c], 1, 1).astype(jnp.bfloat16)
+        for c in range(fan)
+    ]
+    lifted = sum(product(value, leaf_transfer[c]) for c, value in enumerate(values))
+    for c in range(0, fan, 2):
+        coefficients[c // 2] = jnp.concatenate(values[c : c + 2], axis=1)
+    partial[...] += product(lifted.astype(jnp.bfloat16), parent_transfer[0])
+
+
+def lift(density, bases, leaf_transfer, parent_transfer):
+    leaves, rank, width = bases.shape
+    sides = density.shape[0]
     parents = parent_transfer.shape[0]
-    width = bases.shape[2]
-    fan = bases.shape[0] // parents
-    partial[...] = jnp.zeros_like(partial)
-
-    def one_parent(p, _):
-        lifted = jnp.zeros(partial.shape, jnp.float32)
-        held = None
-        for c in range(fan):
-            l = p * fan + c
-            start = pl.multiple_of(l * width, width)
-            value = product(density[:, pl.ds(start, width)], bases[l], 1, 1).astype(jnp.bfloat16)
-            lifted = lifted + product(value, leaf_transfer[l])
-            if c % 2 == 0:
-                held = value
-            else:
-                coefficients[p * (fan // 2) + c // 2] = jnp.concatenate([held, value], axis=1)
-        partial[...] += product(lifted.astype(jnp.bfloat16), parent_transfer[p])
-        return 0
-
-    lax.fori_loop(0, parents, one_parent, 0)
-
-
-def lift(density, bases, leaf_transfer, parent_transfer):
-    leaves, rank, _ = bases.shape
-    sides = density.shape[0]
+    fan = leaves // parents
     return pl.pallas_call(
         lift_kernel,
+        grid=(parents,),
         out_shape=(
             jax.ShapeDtypeStruct((leaves // 2, sides, 2 * rank), jnp.bfloat16),
             jax.ShapeDtypeStruct((sides, rank), jnp.float32),
         ),
-        in_specs=[VMEM] * 4,
-        out_specs=(VMEM, VMEM),
+        in_specs=[
+            pl.BlockSpec((sides, fan * width), lambda p: (0, p)),
+            pl.BlockSpec((fan, rank, width), lambda p: (p, 0, 0)),
+            pl.BlockSpec((fan, rank, rank), lambda p: (p, 0, 0)),
+            pl.BlockSpec((1, rank, rank), lambda p: (p, 0, 0)),
+        ],
+        out_specs=(
+            pl.BlockSpec((fan // 2, sides, 2 * rank), lambda p: (p, 0, 0)),
+            pl.BlockSpec((sides, rank), lambda p: (0, 0)),
+        ),
         compiler_params=PARAMS,
     )(density, bases, leaf_transfer, parent_transfer)
 
@@ -76,7 +84,8 @@
 
 def near_kernel(
     total, place, near_list, near_count, geo_own, geo_low, geo_high, den_own, den_low, den_high,
-    near, task_target, task_source, source, target, density, lhs, column, flux, block,
+    near, task_target, task_source, source, target, density, lhs, column,
+    flux_one, flux_two, block_one, block_two,
 ):
     leaves = geo_own.shape[1]
     width = geo_own.shape[2]
@@ -97,21 +106,21 @@
     def append(t, position):
         live = near_count[t]
         for k in range(slots):
-            s = local(near_list[k, t], first + t, total) + t
+            s = local(near_list[k, t], first, total)
             s = jnp.where(s >= leaves, s + reach, jnp.where(s < 0, s + leaves + reach, s))
             task_source[position] = s
-            task_target[position // 2] = t
+            task_target[position >> 1] = t
             position = position + jnp.where(k < live, 1, 0)
         task_source[position] = everything
-        return (position + 1) // 2 * 2
+        return ((position + 1) >> 1) << 1
 
     for i in range(2):
         task_target[i] = leaves
         task_source[2 * i] = everything
         task_source[2 * i + 1] = everything
     ended = lax.fori_loop(0, leaves, append, 4)
-    pairs = ended // 2 - 2
-    for i in range(2):
+    pairs = (ended >> 1) - 2
+    for i in range(4):
         task_target[pairs + 2 + i] = leaves
         task_source[ended + 2 * i] = everything
         task_source[ended + 2 * i + 1] = everything
@@ -158,22 +167,22 @@
         near[t] = jnp.zeros(near.shape[1:], near.dtype)
         return 0
 
-    lax.fori_loop(0, leaves, prepare, 0)
+    lax.fori_loop(0, leaves, prepare, 0, unroll=8)
     near[leaves] = jnp.zeros(near.shape[1:], near.dtype)
-    block[...] = jnp.zeros_like(block)
-    flux[...] = jnp.zeros_like(flux)
+    for ref in (flux_one, flux_two, block_one, block_two):
+        ref[...] = jnp.zeros_like(ref)
 
     def weights(s):
         high, middle, low = split(get(source, pl.multiple_of(s * 8, 8), 8))
         return jnp.concatenate([high, high, high, middle, middle, low], axis=0).astype(jnp.bfloat16)
 
-    def step(j, _):
-        t = task_target[j]
+    def multiply(j, block):
         both = jnp.concatenate([density[task_source[2 * j + i]] for i in range(2)], axis=1)
-        near[t] += product(both, block[...], 1, 1)
-
-        t = jnp.minimum(task_target[j + 1], leaves - 1)
-        pair = [task_source[2 * j + 2 + i] for i in range(2)]
+        near[task_target[j]] += product(both, block[...], 1, 1)
+
+    def evaluate(j, flux, block):
+        t = jnp.minimum(task_target[j], leaves - 1)
+        pair = [task_source[2 * j + i] for i in range(2)]
         places = [
             jnp.concatenate([get(source, s * 8 + 4 + a, 1) for s in pair], axis=1)
             for a in range(3)
@@ -190,12 +199,22 @@
                 value = flux[r : r + CHUNK, b : b + LANES] * inverse * (inverse * inverse)
                 block[r : r + CHUNK, b : b + LANES] = value.astype(jnp.bfloat16)
 
-        t = jnp.minimum(task_target[j + 2], leaves - 1)
-        pair = [task_source[2 * j + 4 + i] for i in range(2)]
+    def project(j, flux):
+        t = jnp.minimum(task_target[j], leaves - 1)
+        pair = [task_source[2 * j + i] for i in range(2)]
         flux[...] = product(lhs[t], jnp.concatenate([weights(s) for s in pair], axis=1))
+
+    def step(i, _):
+        j = 2 * i
+        multiply(j, block_one)
+        evaluate(j + 1, flux_two, block_two)
+        project(j + 2, flux_one)
+        multiply(j + 1, block_two)
+        evaluate(j + 2, flux_one, block_one)
+        project(j + 3, flux_two)
         return 0
 
-    lax.fori_loop(0, pairs + 2, step, 0)
+    lax.fori_loop(0, (pairs + 3) >> 1, step, 0)
 
 
 def near_field(total, place, near_list, near_count, geometries, densities):
@@ -203,7 +222,7 @@
     everything = leaves + 2 * geometries[1].shape[1]
     sides = densities[0].shape[0]
     slots = near_list.shape[0]
-    most = leaves * (slots // 2 + 1) + 8
+    most = leaves * (slots // 2 + 1) + 16
     return pl.pallas_call(
         functools.partial(near_kernel, total),
         out_shape=jax.ShapeDtypeStruct((leaves + 1, sides, width), jnp.float32),
@@ -218,16 +237,21 @@
             pltpu.VMEM((leaves, width, 48), jnp.bfloat16),
             pltpu.VMEM((leaves, width, 8), jnp.float32),
             pltpu.VMEM((width, 2 * width), jnp.float32),
+            pltpu.VMEM((width, 2 * width), jnp.float32),
+            pltpu.VMEM((width, 2 * width), jnp.bfloat16),
             pltpu.VMEM((width, 2 * width), jnp.bfloat16),
         ],
         compiler_params=PARAMS,
+        cost_estimate=pl.CostEstimate(
+            flops=100 * 10**9 // 2, bytes_accessed=8 * 10**6, transcendentals=3 * 10**7
+        ),
     )(place, near_list, near_count, *geometries, *densities)
 
 
 def final_kernel(
     total, place, far_list, top_far, top_proxies, coupled, coef_own, coef_low, coef_high,
     prox_own, prox_low, prox_high, near, density, bases, leaf_transfer, parent_transfer,
-    out, charges, points, lines, parent_local,
+    out, charges, points, lines, parent_local, far,
 ):
     leaves, rank, width = bases.shape
     first = place[0]
@@ -275,14 +299,14 @@
         for c in range(3, 8):
             lines[pl.ds(g * 8 + c, 8, stride=8), :] = jnp.zeros((8, LANES), jnp.float32)
 
-    def one_leaf(t):
+    def far_leaf(t):
         turned = lines[pl.ds(pl.multiple_of(t * 8, 8), 8), :].T[:rank]
         spread = [jnp.broadcast_to(turned[:, c : c + 1], (rank, LANES)) for c in range(3)]
         blocks = []
         values = []
         for q in range(far_list.shape[0] // 2):
             pair = [
-                local(far_list[2 * q + i, t], first + t, total) + t + leaves for i in range(2)
+                local(far_list[2 * q + i, t], first, total) + leaves for i in range(2)
             ]
             gap = [
                 spread[c]
@@ -294,18 +318,26 @@
             squared = gap[0] * gap[0] + gap[1] * gap[1] + (gap[2] * gap[2] + SOFTEN)
             blocks.append((lax.rsqrt(squared) * (1.0 / FOUR_PI)).astype(jnp.bfloat16))
             values.append(jnp.where(left, charges[pair[0]], charges[pair[1]]))
-        far = product(jnp.concatenate(values, axis=1), jnp.concatenate(blocks, axis=1), 1, 1)
-        leaf_local = far + product(parent_local[t // fan], leaf_transfer[t], 1, 1)
+        far[t] = product(jnp.concatenate(values, axis=1), jnp.concatenate(blocks, axis=1), 1, 1)
+
+    def down_leaf(t, parent):
+        leaf_local = far[t] + product(parent_local[parent], leaf_transfer[t], 1, 1)
         start = pl.multiple_of(t * width, width)
         result = 0.5 * density[:, pl.ds(start, width)].astype(jnp.float32) + near[t]
         out[:, pl.ds(start, width)] = result + product(leaf_local.astype(jnp.bfloat16), bases[t])
 
-    def some(j, _):
-        for i in range(2):
-            one_leaf(2 * j + i)
+    def far_some(j, _):
+        for i in range(FAR_UNROLL):
+            far_leaf(FAR_UNROLL * j + i)
         return 0
 
-    lax.fori_loop(0, leaves // 2, some, 0)
+    def down_some(j, _):
+        for i in range(fan):
+            down_leaf(fan * j + i, j)
+        return 0
+
+    lax.fori_loop(0, leaves // FAR_UNROLL, far_some, 0)
+    lax.fori_loop(0, parents, down_some, 0)
 
 
 def finish(total, place, far_list, top_far, top_proxies, coupled, coefs, proxies, near, density,
@@ -322,6 +354,7 @@
             pltpu.VMEM((3, 3 * leaves, LANES), jnp.float32),
             pltpu.VMEM((leaves * 8, LANES), jnp.float32),
             pltpu.VMEM((parent_transfer.shape[0], sides, rank), jnp.bfloat16),
+            pltpu.VMEM((leaves, sides, rank), jnp.float32),
         ],
         compiler_params=PARAMS,
     )(place, far_list, top_far, top_proxies, coupled, *coefs, *proxies, near, density, bases,
@@ -355,13 +388,13 @@
     prox_high = lax.ppermute(proxies, AXES, backward)
 
     coefficients, partial = lift(density, bases, leaf_transfer, parent_transfer)
-    coef_low = lax.ppermute(coefficients, AXES, forward)
-    coef_high = lax.ppermute(coefficients, AXES, backward)
 
     count = lax.axis_size("sub")
     step = 1
     while step < count:
         partial = partial + lax.ppermute(partial, "sub", [(i, i ^ step) for i in range(count)])
+        if step == 1:
+            partial, geo_low, geo_high = lax.optimization_barrier((partial, geo_low, geo_high))
         step *= 2
     coupled = partial.astype(jnp.bfloat16)[None]
     count = lax.axis_size("leaf")
@@ -369,8 +402,12 @@
     while step < count:
         other = lax.ppermute(coupled, "leaf", [(i, i ^ step) for i in range(count)])
         coupled = jnp.concatenate([coupled, other], axis=0)
+        if step == 1:
+            coupled, den_low, den_high = lax.optimization_barrier((coupled, den_low, den_high))
         step *= 2
 
+    coef_low = lax.ppermute(coefficients, AXES, forward)
+    coef_high = lax.ppermute(coefficients, AXES, backward)
     near = near_field(
         total, place, near_list, near_count,
         (geometry, geo_low, geo_high), (density, den_low, den_high),

time: 188 us -> 161 us (0.86)
  Pallas kernels: 127 us -> 108 us
  starting transfers between devices: 33.4 us -> 26.2 us
  waiting for transfers between devices: 20.9 us -> 16.1 us
  local copies, waits for them, and re-layouts: 8.22 us -> 12.3 us
    pallas_call x1, Pallas kernels: 95.4 us -> 80.8 us  [near_field(): pl.pallas_call(functools.partial(near_kernel, total), out_shape=jax.Shape...]
    ppermute x1, starting transfers between devices: 8.8 us -> 0.01 us  [per_device(): prox_high = lax.ppermute(proxies, AXES, backward)]
    ppermute x1, waiting for transfers between devices: 5.52 us -> 0.01 us  [per_device(): geo_low = lax.ppermute(geometry[:, leaves - reach:], AXES, forward)]
    ppermute x3, waiting for transfers between devices: 8.09 us -> 13.1 us  [per_device(): lax.ppermute(partial, 'sub', [(i, i ^ step) for i in range(count)])]
    ppermute x1, starting transfers between devices: 6.58 us -> 1.67 us  [per_device(): geo_low = lax.ppermute(geometry[:, leaves - reach:], AXES, forward)]
    ppermute x4, waiting for transfers between devices: 7.26 us -> 2.99 us  [per_device(): other = lax.ppermute(coupled, 'leaf', [(i, i ^ step) for i in range(count)])]
    pallas_call x1, Pallas kernels: 26.6 us -> 23 us  [finish(): pl.pallas_call(functools.partial(final_kernel, total), out_shape=jax.Shap...]
    unnamed x35 -> x42, local copies, waits for them, and re-layouts: 6.38 us -> 9.86 us
  transfers between devices with their start and end apart: 15 -> 15, of which waited for: 6 -> 5; matrix products, arithmetic and copies ran while one was open for 1% -> 1% of each run, Pallas kernels for 50% -> 52%
where the time goes in v2:
time: 161 us; the launch traced here: 163 us
  Pallas kernels  108 us (67%)
  starting transfers between devices  26.2 us (16%)
  waiting for transfers between devices  16.1 us (10%)
  local copies, waits for them, and re-layouts  12.3 us (8%)
    pallas_call x1, Pallas kernels, near_field(): pl.pallas_call(functools.partial(near_kernel, total), out_shape=jax.Shape...  80.8 us
    pallas_call x1, Pallas kernels, finish(): pl.pallas_call(functools.partial(final_kernel, total), out_shape=jax.Shap...  23 us
    ppermute x3, waiting for transfers between devices, per_device(): lax.ppermute(partial, 'sub', [(i, i ^ step) for i in range(count)])  13.1 us
    unnamed x42, local copies, waits for them, and re-layouts  9.86 us
    ppermute x3, starting transfers between devices, per_device(): lax.ppermute(partial, 'sub', [(i, i ^ step) for i in range(count)])  7.18 us
    ppermute x1, starting transfers between devices, per_device(): den_high = lax.ppermute(density[:, :reach * width], AXES, backward)  6.62 us
    ppermute x4, starting transfers between devices, per_device(): other = lax.ppermute(coupled, 'leaf', [(i, i ^ step) for i in range(count)])  6.21 us
    pallas_call x1, Pallas kernels, lift(): pl.pallas_call(lift_kernel, grid=(parents,), out_shape=(jax.ShapeDtypeStr...  3.86 us
  transfers between devices with their start and end apart: 15, of which 5 were waited for; matrix products, arithmetic and copies ran while one was open for 1% of the time, Pallas kernels for 52%

profile of v2, /device:TPU:8, one launch (start us, length us, event | category | flops | bytes accessed | tf_op | source)
XLA Modules:
  0.0 162.6 jit_solution(4596496501542276376)
XLA Ops:
  0.0 1.2 fusion.2
  1.6 1.7 %collective-permute-start.1 = (f32[6,32,256]{2,1,0:T(8,128)S(1)}, f32[6,32,256]{2,1,0:T(8,128)S(1)}, u32[]{:S(2)}, u32[]{:S(2)}) collective-permute-start(f32[6,32,256]{2,1,0:T(8,128)S(1)} %get-tuple-element.24), channel_id=1, source_target_pairs={{0,1},{1,2},{2,3},{3,4},{4,5},{5,6},{6,7},{7,8},{8,9},{9,10},{10,1... | collective-permute-start | bytes 589832 | tf_op jit(solution)/shard_map/ppermute | solution.py:383
  3.3 1.3 fusion.1
  4.6 6.6 %collective-permute-start.7 = (bf16[32,8192]{1,0:T(8,128)(2,1)S(1)}, bf16[32,8192]{1,0:T(8,128)(2,1)S(1)}, u32[]{:S(2)}, u32[]{:S(2)}) collective-permute-start(bf16[32,8192]{1,0:T(8,128)(2,1)S(1)} %get-tuple-element.21), channel_id=1, source_target_pairs={{1,0},{2,1},{3,2},{4,3},{5,4},{6,5},{7,6},{8,7},{9,8},{10,9},{11,1... | collective-permute-start | bytes 1572872 | tf_op jit(solution)/shard_map/ppermute | solution.py:386
  11.2 1.6 copy-done.1
  12.8 3.9 %shard_map.109 = (bf16[32,32,128]{2,1,0:T(8,128)(2,1)S(1)}, f32[32,64]{1,0:T(8,128)S(1)}) custom-call(bf16[32,16384]{1,0:T(8,128)(2,1)S(1)} %copy-done, bf16[64,64,256]{2,1,0:T(8,128)(2,1)S(1)} %copy-done.1, bf16[64,64,64]{2,1,0:T(8,128)(2,1)S(1)} %copy-done.3, bf16[8,64,64]{2,1,0:T(8,128)(2,1)S(1)} %copy-done.5), custom_call_target="tpu_custom_call" | custom-call | tf_op jit(solution)/shard_map/pallas_call | solution.py:57
  16.7 7.2 %collective-permute-start = (f32[32,64]{1,0:T(8,128)S(1)}, f32[32,64]{1,0:T(8,128)S(1)}, u32[]{:S(2)}, u32[]{:S(2)}) collective-permute-start(f32[32,64]{1,0:T(8,128)S(1)} %get-tuple-element.13), channel_id=1, source_target_pairs={{0,1},{1,0},{2,3},{3,2},{4,5},{5,4},{6,7},{7,6},{8,9},{9,8},{10,11... | collective-permute-start | bytes 24584 | tf_op jit(solution)/shard_map/ppermute | solution.py:395
  23.9 2.6 %collective-permute-done = f32[32,64]{1,0:T(8,128)S(1)} collective-permute-done((f32[32,64]{1,0:T(8,128)S(1)}, f32[32,64]{1,0:T(8,128)S(1)}, u32[]{:S(2)}, u32[]{:S(2)}) %collective-permute-start) | collective-permute-done | bytes 8224 | tf_op jit(solution)/shard_map/ppermute | solution.py:395
  27.9 5.2 %collective-permute-done.3 = f32[32,64]{1,0:T(8,128)S(1)} collective-permute-done((f32[32,64]{1,0:T(8,128)S(1)}, f32[32,64]{1,0:T(8,128)S(1)}, u32[]{:S(2)}, u32[]{:S(2)}) %collective-permute-start.3) | collective-permute-done | bytes 8224 | tf_op jit(solution)/shard_map/ppermute | solution.py:395
  33.1 5.2 %collective-permute-done.4 = f32[32,64]{1,0:T(8,128)S(1)} collective-permute-done((f32[32,64]{1,0:T(8,128)S(1)}, f32[32,64]{1,0:T(8,128)S(1)}, u32[]{:S(2)}, u32[]{:S(2)}) %collective-permute-start.4) | collective-permute-done | bytes 8224 | tf_op jit(solution)/shard_map/ppermute | solution.py:395
  38.4 1.2 collective-permute-done.5
  40.4 0.8 copy-done.13
  41.2 1.9 %collective-permute-start.8 = (bf16[2,32,64]{2,1,0:T(8,128)(2,1)S(1)}, bf16[2,32,64]{2,1,0:T(8,128)(2,1)S(1)}, u32[]{:S(2)}, u32[]{:S(2)}) collective-permute-start(bf16[2,32,64]{2,1,0:T(8,128)(2,1)S(1)} %pad_maximum_fusion.3), channel_id=1, source_target_pairs={{0,16},{8,24},{16,0},{24,8},{32,48},{40,56},{48,32},{56,40},{64,80... | collective-permute-start | bytes 24584 | tf_op jit(solution)/shard_map/ppermute | solution.py:403
  43.1 2.0 %collective-permute-start.13 = (f32[3,64,64]{2,1,0:T(8,128)S(1)}, f32[3,64,64]{2,1,0:T(8,128)}, u32[]{:S(2)}, u32[]{:S(2)}) collective-permute-start(f32[3,64,64]{2,1,0:T(8,128)S(1)} %bitcast.13), channel_id=1, source_target_pairs={{0,1},{1,2},{2,3},{3,4},{4,5},{5,6},{6,7},{7,8},{8,9},{9,10},{10,1... | collective-permute-start | bytes 147464 | tf_op jit(solution)/shard_map/ppermute | solution.py:387
  45.1 1.4 collective-permute-start.12
  47.1 3.7 %collective-permute-start.9 = (bf16[4,32,64]{2,1,0:T(8,128)(2,1)S(1)}, bf16[4,32,64]{2,1,0:T(8,128)(2,1)S(1)}, u32[]{:S(2)}, u32[]{:S(2)}) collective-permute-start(bf16[4,32,64]{2,1,0:T(8,128)(2,1)S(1)} %pad_maximum_fusion.2), channel_id=1, source_target_pairs={{0,32},{8,40},{16,48},{24,56},{32,0},{40,8},{48,16},{56,24},{64,96... | collective-permute-start | bytes 49160 | tf_op jit(solution)/shard_map/ppermute | solution.py:403
  50.9 1.8 %collective-permute-done.9 = bf16[4,32,64]{2,1,0:T(8,128)(2,1)S(1)} collective-permute-done((bf16[4,32,64]{2,1,0:T(8,128)(2,1)S(1)}, bf16[4,32,64]{2,1,0:T(8,128)(2,1)S(1)}, u32[]{:S(2)}, u32[]{:S(2)}) %collective-permute-start.9) | collective-permute-done | bytes 16416 | tf_op jit(solution)/shard_map/ppermute | solution.py:403
  53.4 1.0 copy-done.12
  54.4 1.0 copy-done.14
  55.5 0.9 copy-done.16
  56.4 0.9 copy-done.18
  57.3 80.8 %shard_map.110.near = f32[65,32,256]{2,1,0:T(8,128)S(1)} custom-call(s32[2]{0:T(128)S(1)} %pad_add_fusion.place, s32[9,64]{1,0:T(8,128)S(1)} %bitcast.18, s32[64]{0:T(128)S(1)} %copy-done.20, f32[6,64,256]{2,1,0:T(8,128)S(1)} %bitcast.11, f32[6,32,256]{2,1,0:T(8,128)S(1)} %copy-done.18, f32[6,32,256]{2,1,0:T(8,128)S(1)} %copy-done.16, ...), custom_call_target="tpu_custom_call" | custom-call | flops 49999998976 | bytes 8000000 | tf_op jit(solution)/shard_map/pallas_call | solution.py:226
  138.1 1.4 copy-done.4
  139.6 23.0 %shard_map.111 = f32[32,16384]{1,0:T(8,128)} custom-call(s32[2]{0:T(128)S(1)} %pad_add_fusion.place, s32[16,64]{1,0:T(8,128)S(1)} %bitcast.16, s32[8,16]{1,0:T(8,128)S(1)} %bitcast.17, f32[3,16,64]{2,1,0:T(8,128)S(1)} %bitcast.15, bf16[16,32,64]{2,1,0:T(8,128)(2,1)S(1)} %pad_maximum_fusion.coupled, bf16[32,32,128]{2,1,0:T(8,128)(2,1)S(1)} %get-tuple-element.16.coef_own, ...), custom_call_target="tpu_custom_call" | custom-call | tf_op jit(solution)/shard_map/pallas_call | solution.py:347
  (61 shorter events, 4.1 us)
Async XLA Ops:
  0.0 11.2 %copy-start.3 = (bf16[64,64,64]{2,1,0:T(8,128)(2,1)S(1)}, bf16[64,64,64]{2,1,0:T(8,128)(2,1)}, u32[]{:S(2)}) copy-start(bf16[64,64,64]{2,1,0:T(8,128)(2,1)} %leaf_transfer.3) | copy-start | bytes 1572868
  1.2 25.3 %collective-permute-start.2 = (f32[6,32,256]{2,1,0:T(8,128)S(1)}, f32[6,32,256]{2,1,0:T(8,128)S(1)}, u32[]{:S(2)}, u32[]{:S(2)}) collective-permute-start(f32[6,32,256]{2,1,0:T(8,128)S(1)} %get-tuple-element.23), channel_id=1, source_target_pairs={{1,0},{2,1},{3,2},{4,3},{5,4},{6,5},{7,6},{8,7},{9,8},{10,9},{11,1... | collective-permute-start | bytes 589832 | tf_op jit(solution)/shard_map/ppermute | solution.py:384
  1.6 25.6 %collective-permute-start.1 = (f32[6,32,256]{2,1,0:T(8,128)S(1)}, f32[6,32,256]{2,1,0:T(8,128)S(1)}, u32[]{:S(2)}, u32[]{:S(2)}) collective-permute-start(f32[6,32,256]{2,1,0:T(8,128)S(1)} %get-tuple-element.24), channel_id=1, source_target_pairs={{0,1},{1,2},{2,3},{3,4},{4,5},{5,6},{6,7},{7,8},{8,9},{9,10},{10,1... | collective-permute-start | bytes 589832 | tf_op jit(solution)/shard_map/ppermute | solution.py:383
  4.6 35.0 %collective-permute-start.7 = (bf16[32,8192]{1,0:T(8,128)(2,1)S(1)}, bf16[32,8192]{1,0:T(8,128)(2,1)S(1)}, u32[]{:S(2)}, u32[]{:S(2)}) collective-permute-start(bf16[32,8192]{1,0:T(8,128)(2,1)S(1)} %get-tuple-element.21), channel_id=1, source_target_pairs={{1,0},{2,1},{3,2},{4,3},{5,4},{6,5},{7,6},{8,7},{9,8},{10,9},{11,1... | collective-permute-start | bytes 1572872 | tf_op jit(solution)/shard_map/ppermute | solution.py:386
  11.2 29.2 %collective-permute-start.6 = (bf16[32,8192]{1,0:T(8,128)(2,1)S(1)}, bf16[32,8192]{1,0:T(8,128)(2,1)S(1)}, u32[]{:S(2)}, u32[]{:S(2)}) collective-permute-start(bf16[32,8192]{1,0:T(8,128)(2,1)S(1)} %get-tuple-element.22), channel_id=1, source_target_pairs={{0,1},{1,2},{2,3},{3,4},{4,5},{5,6},{6,7},{7,8},{8,9},{9,10},{10,1... | collective-permute-start | bytes 1572872 | tf_op jit(solution)/shard_map/ppermute | solution.py:385
  12.8 30.2 %copy-start.7 = (f32[64,3,64]{2,0,1:T(8,128)S(1)}, f32[64,3,64]{2,0,1:T(8,128)}, u32[]{:S(2)}) copy-start(f32[64,3,64]{2,0,1:T(8,128)} %param.17) | copy-start | bytes 147460
  12.8 40.6 %copy-start.6 = (f32[64,6,256]{2,0,1:T(8,128)S(1)}, f32[64,6,256]{2,0,1:T(8,128)}, u32[]{:S(2)}) copy-start(f32[64,6,256]{2,0,1:T(8,128)} %param.12) | copy-start | bytes 1179652
  12.8 40.6 %copy-start.19 = (s32[64,9]{0,1:T(8,128)S(1)}, s32[64,9]{0,1:T(8,128)}, u32[]{:S(2)}) copy-start(s32[64,9]{0,1:T(8,128)} %param.13) | copy-start | bytes 6916
  12.8 40.6 %copy-start.20 = (s32[64]{0:T(128)S(1)}, s32[64]{0:T(128)}, u32[]{:S(2)}) copy-start(s32[64]{0:T(128)} %near_count.1) | copy-start | bytes 772
  16.7 9.8 %collective-permute-start = (f32[32,64]{1,0:T(8,128)S(1)}, f32[32,64]{1,0:T(8,128)S(1)}, u32[]{:S(2)}, u32[]{:S(2)}) collective-permute-start(f32[32,64]{1,0:T(8,128)S(1)} %get-tuple-element.13), channel_id=1, source_target_pairs={{0,1},{1,0},{2,3},{3,2},{4,5},{5,4},{6,7},{7,6},{8,9},{9,8},{10,11... | collective-permute-start | bytes 24584 | tf_op jit(solution)/shard_map/ppermute | solution.py:395
  27.9 5.2 %collective-permute-start.3 = (f32[32,64]{1,0:T(8,128)S(1)}, f32[32,64]{1,0:T(8,128)S(1)}, u32[]{:S(2)}, u32[]{:S(2)}) collective-permute-start(f32[32,64]{1,0:T(8,128)S(1)} %add.13), channel_id=1, source_target_pairs={{0,2},{1,3},{2,0},{3,1},{4,6},{5,7},{6,4},{7,5},{8,10},{9,11},{10,... | collective-permute-start | bytes 24584 | tf_op jit(solution)/shard_map/ppermute | solution.py:395
  33.1 5.2 %collective-permute-start.4 = (f32[32,64]{1,0:T(8,128)S(1)}, f32[32,64]{1,0:T(8,128)S(1)}, u32[]{:S(2)}, u32[]{:S(2)}) collective-permute-start(f32[32,64]{1,0:T(8,128)S(1)} %add.14), channel_id=1, source_target_pairs={{0,4},{1,5},{2,6},{3,7},{4,0},{5,1},{6,2},{7,3},{8,12},{9,13},{10,... | collective-permute-start | bytes 24584 | tf_op jit(solution)/shard_map/ppermute | solution.py:395
  38.4 1.2 collective-permute-start.5
  41.2 5.9 %collective-permute-start.8 = (bf16[2,32,64]{2,1,0:T(8,128)(2,1)S(1)}, bf16[2,32,64]{2,1,0:T(8,128)(2,1)S(1)}, u32[]{:S(2)}, u32[]{:S(2)}) collective-permute-start(bf16[2,32,64]{2,1,0:T(8,128)(2,1)S(1)} %pad_maximum_fusion.3), channel_id=1, source_target_pairs={{0,16},{8,24},{16,0},{24,8},{32,48},{40,56},{48,32},{56,40},{64,80... | collective-permute-start | bytes 24584 | tf_op jit(solution)/shard_map/ppermute | solution.py:403
  43.1 96.5 %collective-permute-start.14 = (f32[3,64,64]{2,1,0:T(8,128)S(1)}, f32[3,64,64]{2,1,0:T(8,128)}, u32[]{:S(2)}, u32[]{:S(2)}) collective-permute-start(f32[3,64,64]{2,1,0:T(8,128)S(1)} %bitcast.12), channel_id=1, source_target_pairs={{1,0},{2,1},{3,2},{4,3},{5,4},{6,5},{7,6},{8,7},{9,8},{10,9},{11,1... | collective-permute-start | bytes 147464 | tf_op jit(solution)/shard_map/ppermute | solution.py:388
  43.1 96.5 %collective-permute-start.13 = (f32[3,64,64]{2,1,0:T(8,128)S(1)}, f32[3,64,64]{2,1,0:T(8,128)}, u32[]{:S(2)}, u32[]{:S(2)}) collective-permute-start(f32[3,64,64]{2,1,0:T(8,128)S(1)} %bitcast.13), channel_id=1, source_target_pairs={{0,1},{1,2},{2,3},{3,4},{4,5},{5,6},{6,7},{7,8},{8,9},{9,10},{10,1... | collective-permute-start | bytes 147464 | tf_op jit(solution)/shard_map/ppermute | solution.py:387
  45.1 94.5 %collective-permute-start.12 = (bf16[32,32,128]{2,1,0:T(8,128)(2,1)S(1)}, bf16[32,32,128]{2,1,0:T(8,128)(2,1)S(1)}, u32[]{:S(2)}, u32[]{:S(2)}) collective-permute-start(bf16[32,32,128]{2,1,0:T(8,128)(2,1)S(1)} %get-tuple-element.16.coef_own), channel_id=1, source_target_pairs={{1,0},{2,1},{3,2},{4,3},{5,4},{6,5},{7,6},{8,7},{9,8},{10,9},{11,1... | collective-permute-start | bytes 786440 | tf_op jit(solution)/shard_map/ppermute | solution.py:410
  46.5 93.0 %collective-permute-start.11 = (bf16[32,32,128]{2,1,0:T(8,128)(2,1)S(1)}, bf16[32,32,128]{2,1,0:T(8,128)(2,1)S(1)}, u32[]{:S(2)}, u32[]{:S(2)}) collective-permute-start(bf16[32,32,128]{2,1,0:T(8,128)(2,1)S(1)} %get-tuple-element.16.coef_own), channel_id=1, source_target_pairs={{0,1},{1,2},{2,3},{3,4},{4,5},{5,6},{6,7},{7,8},{8,9},{9,10},{10,1... | collective-permute-start | bytes 786440 | tf_op jit(solution)/shard_map/ppermute | solution.py:409
  47.1 5.6 %collective-permute-start.9 = (bf16[4,32,64]{2,1,0:T(8,128)(2,1)S(1)}, bf16[4,32,64]{2,1,0:T(8,128)(2,1)S(1)}, u32[]{:S(2)}, u32[]{:S(2)}) collective-permute-start(bf16[4,32,64]{2,1,0:T(8,128)(2,1)S(1)} %pad_maximum_fusion.2), channel_id=1, source_target_pairs={{0,32},{8,40},{16,48},{24,56},{32,0},{40,8},{48,16},{56,24},{64,96... | collective-permute-start | bytes 49160 | tf_op jit(solution)/shard_map/ppermute | solution.py:403
  52.7 86.8 %collective-permute-start.10 = (bf16[8,32,64]{2,1,0:T(8,128)(2,1)S(1)}, bf16[8,32,64]{2,1,0:T(8,128)(2,1)S(1)}, u32[]{:S(2)}, u32[]{:S(2)}) collective-permute-start(bf16[8,32,64]{2,1,0:T(8,128)(2,1)S(1)} %pad_maximum_fusion.1), channel_id=1, source_target_pairs={{0,64},{8,72},{16,80},{24,88},{32,96},{40,104},{48,112},{56,120},{... | collective-permute-start | bytes 98312 | tf_op jit(solution)/shard_map/ppermute | solution.py:403
  57.3 82.2 %copy-start.2 = (bf16[64,64,256]{2,1,0:T(8,128)(2,1)S(1)}, bf16[64,64,256]{2,1,0:T(8,128)(2,1)}, u32[]{:S(2)}) copy-start(bf16[64,64,256]{2,1,0:T(8,128)(2,1)} %bases.3) | copy-start | bytes 6291460
  57.3 82.2 %copy-start.8 = (f32[16,3,64]{2,0,1:T(8,128)S(1)}, f32[16,3,64]{2,0,1:T(8,128)}, u32[]{:S(2)}) copy-start(f32[16,3,64]{2,0,1:T(8,128)} %param.20) | copy-start | bytes 36868
  57.3 82.3 %copy-start.9 = (s32[64,16]{0,1:T(8,128)S(1)}, s32[64,16]{0,1:T(8,128)}, u32[]{:S(2)}) copy-start(s32[64,16]{0,1:T(8,128)} %param.15) | copy-start | bytes 12292
  57.3 82.3 %copy-start.10 = (s32[16,8]{0,1:T(8,128)S(1)}, s32[16,8]{0,1:T(8,128)}, u32[]{:S(2)}) copy-start(s32[16,8]{0,1:T(8,128)} %param.21) | copy-start | bytes 1540
  (12 other events, 32.3 us)
